TPU v7x, 256 devices: a whole 4x4x8 slice. The times are simulated.
256 devices in a mesh: dp: 32 (over x, y, core), tensor: 8 (over z).
Axes of the slice: x: 4, y: 4, z: 8, core: 2. Of those that a mesh axis runs over, the one named last changes fastest.
Arguments:
- queries: bfloat16 [4096, 8192], P('dp', 'tensor'), may hold values from -6 to 6
- resp_kv: bfloat16 [4096, 8, 256], P('dp', 'tensor'), may hold values from -6 to 6
- prompt_kv: bfloat16 [8192, 8, 256], P(('dp', 'tensor')), may hold values from -6 to 6
- resp_prompt: int32 [32, 4], P('dp'), may hold values from 0 to 7
- row_segment: int32 [32, 128], P('dp'), may hold values from 0 to 3, never falling along the last dimension, each value on 1 to 64 neighbouring positions
- cotangent: bfloat16 [4096, 8192], P('dp', 'tensor'), may hold values from -6 to 6
Outputs:
- attended: bfloat16 [4096, 8192], P('dp', 'tensor')
- query_grad: bfloat16 [4096, 8192], P('dp', 'tensor')
- resp_kv_grad: bfloat16 [4096, 8, 256], P('dp', 'tensor')
- prompt_kv_grad: float32 [8192, 8, 256], P(('dp', 'tensor'))
Inputs may be any that keep to these rules, and one draw needn't show every extreme that they name: `row_segment`: in each block of 128 tokens, response numbers never fall and each of the 4 responses holds 1 to 64 tokens.
All inputs are finite; a program needn't handle non-finite values.
Results may differ from a plain program's by a relative error of at most 0.017.
Values may be sent and summed in bfloat16 or wider, within the bound.
A program may use at most 128 MiB of HBM per device.

v0:
```python
import math

import jax
import jax.numpy as jnp
from jax import lax
from jax.sharding import PartitionSpec as P

PLEN = 1024


def block_attention(queries, resp_kv, prompt_all, resp_prompt, row_segment, cotangent, prompt_len):
    row_count = queries.shape[0]
    kv_groups = resp_kv.shape[1]
    head_width = resp_kv.shape[2] // 2
    grouped = queries.shape[1] // (kv_groups * head_width)
    score_scale = 1.0 / math.sqrt(head_width)
    window = row_count // 2
    q_heads = queries.reshape(row_count, kv_groups, grouped, head_width)
    g_heads = cotangent.reshape(row_count, kv_groups, grouped, head_width)
    resp_keys = resp_kv[..., :head_width]
    resp_vals = resp_kv[..., head_width:]
    position = jnp.arange(row_count, dtype=jnp.int32)
    self_mask = (row_segment[:, None] == row_segment[None, :]) & (
        position[None, :] <= position[:, None]
    )
    self_scores = (
        jnp.einsum("rkgd,jkd->kgrj", q_heads, resp_keys, preferred_element_type=jnp.float32)
        * score_scale
    )
    self_scores = jnp.where(self_mask[None, None], self_scores, -1e30)
    resp_count = resp_prompt.shape[0]
    seg_ids = jnp.arange(resp_count, dtype=jnp.int32)
    starts = jnp.sum((row_segment[None, :] < seg_ids[:, None]).astype(jnp.int32), axis=1)
    starts = jnp.minimum(starts, row_count - window)
    prompt_scores = []
    prompt_pieces = []
    full_max = jnp.max(self_scores, axis=-1)
    for seg in range(resp_count):
        start = starts[seg]
        seg_window = lax.dynamic_slice_in_dim(row_segment, start, window, 0)
        live = seg_window == seg
        q_window = lax.dynamic_slice_in_dim(q_heads, start, window, 0)
        offset = resp_prompt[seg] * prompt_len
        piece = lax.dynamic_slice_in_dim(prompt_all, offset, prompt_len, 0)
        scores_now = (
            jnp.einsum(
                "rkgd,jkd->kgrj",
                q_window,
                piece[..., :head_width],
                preferred_element_type=jnp.float32,
            )
            * score_scale
        )
        scores_now = jnp.where(live[None, None, :, None], scores_now, -1e30)
        window_max = jnp.max(scores_now, axis=-1)
        placed_max = lax.dynamic_update_slice_in_dim(
            jnp.full(full_max.shape, -1e30, jnp.float32), window_max, start, 2
        )
        placed_live = lax.dynamic_update_slice_in_dim(
            jnp.zeros((row_count,), jnp.bool_), live, start, 0
        )
        full_max = jnp.where(
            placed_live[None, None, :], jnp.maximum(full_max, placed_max), full_max
        )
        prompt_scores.append(scores_now)
        prompt_pieces.append((start, offset, q_window, piece))
    total = jnp.sum(jnp.exp(self_scores - full_max[..., None]), axis=-1)
    for seg in range(resp_count):
        start = prompt_pieces[seg][0]
        max_window = lax.dynamic_slice_in_dim(full_max, start, window, 2)
        part_total = jnp.sum(jnp.exp(prompt_scores[seg] - max_window[..., None]), axis=-1)
        total = total + lax.dynamic_update_slice_in_dim(jnp.zeros_like(total), part_total, start, 2)
    lse = full_max + jnp.log(total)
    self_probs = jnp.exp(self_scores - lse[..., None]).astype(jnp.bfloat16)
    out = jnp.einsum("kgrj,jkd->kgrd", self_probs, resp_vals, preferred_element_type=jnp.float32)
    prompt_probs = []
    for seg in range(resp_count):
        start, offset, q_window, piece = prompt_pieces[seg]
        lse_window = lax.dynamic_slice_in_dim(lse, start, window, 2)
        probs_now = jnp.exp(prompt_scores[seg] - lse_window[..., None]).astype(jnp.bfloat16)
        out_window = jnp.einsum(
            "kgrj,jkd->kgrd", probs_now, piece[..., head_width:], preferred_element_type=jnp.float32
        )
        out = out + lax.dynamic_update_slice_in_dim(jnp.zeros_like(out), out_window, start, 2)
        prompt_probs.append(probs_now)
    attended = out.transpose(2, 0, 1, 3).reshape(row_count, -1)
    g_float = g_heads.astype(jnp.float32).transpose(1, 2, 0, 3)
    row_delta = jnp.sum(g_float * out, axis=-1)
    self_dprob = jnp.einsum(
        "rkgd,jkd->kgrj", g_heads, resp_vals, preferred_element_type=jnp.float32
    )
    self_dscore = (
        self_probs.astype(jnp.float32) * (self_dprob - row_delta[..., None]) * score_scale
    ).astype(jnp.bfloat16)
    query_grad = jnp.einsum(
        "kgrj,jkd->rkgd", self_dscore, resp_keys, preferred_element_type=jnp.float32
    )
    key_grad = jnp.einsum(
        "kgrj,rkgd->jkd", self_dscore, q_heads, preferred_element_type=jnp.float32
    )
    value_grad = jnp.einsum(
        "kgrj,rkgd->jkd", self_probs, g_heads, preferred_element_type=jnp.float32
    )
    prompt_grad = jnp.zeros(prompt_all.shape, jnp.float32)
    for seg in range(resp_count):
        start, offset, q_window, piece = prompt_pieces[seg]
        probs_now = prompt_probs[seg]
        g_window = lax.dynamic_slice_in_dim(g_heads, start, window, 0)
        delta_window = lax.dynamic_slice_in_dim(row_delta, start, window, 2)
        dprob_now = jnp.einsum(
            "rkgd,jkd->kgrj", g_window, piece[..., head_width:], preferred_element_type=jnp.float32
        )
        dscore_now = (
            probs_now.astype(jnp.float32) * (dprob_now - delta_window[..., None]) * score_scale
        ).astype(jnp.bfloat16)
        query_part = jnp.einsum(
            "kgrj,jkd->rkgd",
            dscore_now,
            piece[..., :head_width],
            preferred_element_type=jnp.float32,
        )
        query_grad = query_grad + lax.dynamic_update_slice_in_dim(
            jnp.zeros_like(query_grad), query_part, start, 0
        )
        key_part = jnp.einsum(
            "kgrj,rkgd->jkd", dscore_now, q_window, preferred_element_type=jnp.float32
        )
        value_part = jnp.einsum(
            "kgrj,rkgd->jkd", probs_now, g_window, preferred_element_type=jnp.float32
        )
        current = lax.dynamic_slice_in_dim(prompt_grad, offset, prompt_len, 0)
        prompt_grad = lax.dynamic_update_slice_in_dim(
            prompt_grad, current + jnp.concatenate([key_part, value_part], axis=-1), offset, 0
        )
    resp_grad = jnp.concatenate([key_grad, value_grad], axis=-1)
    return (attended, query_grad.reshape(row_count, -1), resp_grad, prompt_grad)


def local(queries, resp_kv, prompt_kv, resp_prompt, row_segment, cotangent):
    regrouped = lax.all_to_all(prompt_kv, "tensor", split_axis=1, concat_axis=0, tiled=True)
    whole_prompt = lax.all_gather(regrouped, "dp", axis=0, tiled=True)
    attended, query_grad, resp_grad, prompt_grad = block_attention(
        queries, resp_kv, whole_prompt, resp_prompt[0], row_segment[0], cotangent, PLEN
    )
    summed = lax.psum_scatter(
        prompt_grad.astype(jnp.bfloat16), "dp", scatter_dimension=0, tiled=True
    ).astype(jnp.float32)
    prompt_kv_grad = lax.all_to_all(
        summed.astype(jnp.bfloat16), "tensor", split_axis=0, concat_axis=1, tiled=True
    ).astype(summed.dtype)
    return (
        attended.astype(jnp.bfloat16),
        query_grad.astype(jnp.bfloat16),
        resp_grad.astype(jnp.bfloat16),
        prompt_kv_grad,
    )


def solution(mesh):
    return jax.shard_map(
        local,
        mesh=mesh,
        in_specs=(
            P("dp", "tensor"),
            P("dp", "tensor", None),
            P(("dp", "tensor"), None, None),
            P("dp", None),
            P("dp", None),
            P("dp", "tensor"),
        ),
        out_specs=(
            P("dp", "tensor"),
            P("dp", "tensor"),
            P("dp", "tensor", None),
            P(("dp", "tensor"), None, None),
        ),
        check_vma=False,
    )
```

profile of v0, /device:TPU:2, one launch (start us, length us, event | category | flops | bytes accessed | tf_op | source)
XLA Modules:
  0.0 252.7 jit_solution(3390372640366192466)
XLA Ops:
  7.2 1.0 copy.79
  8.2 17.5 %all_to_all.27 = bf16[32,8,256]{2,0,1:T(8,128)(2,1)} all-to-all(bf16[32,8,256]{2,0,1:T(8,128)(2,1)S(1)} %copy.79), channel_id=1, replica_groups=mesh['dp'=32,'tensor'=8] {'tensor'}, dimensions={1} | all-to-all | bytes 262144 | tf_op jit(solution)/shard_map/all_to_all | solution.py:140
  25.8 0.8 convert_reduce_fusion
  26.5 0.7 fusion.126
  32.4 1.5 fusion.125
  36.5 1.1 copy.114
  37.6 0.9 copy.88
  38.5 1.1 copy.113
  43.8 29.1 %all-gather.2.cloned.1.call-done = bf16[8192,1,256]{2,0,1:T(8,128)(2,1)} async-done(((bf16[256,1,256]{2,0,1:T(8,128)(2,1)}), bf16[8192,1,256]{2,0,1:T(8,128)(2,1)}) %all-gather.2.cloned.1.call-update) | async-done | bytes 4194320 | tf_op jit(solution)/shard_map/all_gather | solution.py:141
  73.0 1.5 bitcast_reduce_fusion.3
  74.7 2.8 %bitcast_reduce_fusion.1 = (f32[8,64]{1,0:T(8,128)S(1)}, f32[1,1024,64,8]{1,2,3,0:T(8,128)}) fusion(bf16[64,1,8,128]{3,2,0,1:T(8,128)(2,1)S(1)} %get-tuple-element.23, bf16[8192,1,256]{2,0,1:T(8,128)(2,1)} %all-gather.2.cloned.1.call-done, s32[]{:T(128)S(6)} %select_n.126, pred[64]{0:T(512)(128)(4,1)S(1)} %get-tuple-element.43), kind=kOutput, calls=%fused_computation.26 | convolution fusion | flops 135790080 | bytes 2492484 | tf_op jit(solution)/shard_map/rkgd,jkd->kgrj/dot_general | solution.py:46
  77.6 2.8 %bitcast_reduce_fusion.2 = (f32[8,64]{1,0:T(8,128)S(1)}, f32[1,1024,64,8]{1,2,3,0:T(8,128)}) fusion(bf16[64,1,8,128]{3,2,0,1:T(8,128)(2,1)S(1)} %get-tuple-element.24, bf16[8192,1,256]{2,0,1:T(8,128)(2,1)} %all-gather.2.cloned.1.call-done, s32[]{:T(128)S(6)} %select_n.122, pred[64]{0:T(512)(128)(4,1)S(1)} %get-tuple-element.45), kind=kOutput, calls=%fused_computation.34 | convolution fusion | flops 135790080 | bytes 2492484 | tf_op jit(solution)/shard_map/rkgd,jkd->kgrj/dot_general | solution.py:46
  80.5 2.8 %bitcast_reduce_fusion = (f32[8,64]{1,0:T(8,128)S(1)}, f32[1,1024,64,8]{1,2,3,0:T(8,128)}) fusion(bf16[64,1,8,128]{3,2,0,1:T(8,128)(2,1)S(1)} %get-tuple-element.25, bf16[8192,1,256]{2,0,1:T(8,128)(2,1)} %all-gather.2.cloned.1.call-done, s32[]{:T(128)S(6)} %select_n.130, pred[64]{0:T(512)(128)(4,1)S(1)} %get-tuple-element.44), kind=kOutput, calls=%fused_computation.18 | convolution fusion | flops 135790080 | bytes 2492484 | tf_op jit(solution)/shard_map/rkgd,jkd->kgrj/dot_general | solution.py:46
  83.7 2.3 fusion.21
  86.5 3.0 %fusion.13 = (f32[8,64]{1,0:T(8,128)S(1)}, f32[8,64]{1,0:T(8,128)S(1)}) fusion(f32[1,1024,64,8]{1,2,3,0:T(8,128)} %get-tuple-element.51, f32[8,64]{1,0:T(8,128)S(1)} %get-tuple-element.34, f32[8,64]{1,0:T(8,128)S(1)} %get-tuple-element.35, f32[1,1024,64,8]{1,2,3,0:T(8,128)} %get-tuple-element.53), kind=kLoop, calls=%fused_computation.20 | loop fusion | flops 2096128 | bytes 4202496 | tf_op jit(solution)/shard_map/reduce_sum | solution.py:71
  90.3 0.4 fusion.27
  90.6 1.1 copy-done.1
  91.8 0.4 fusion.23
  92.1 0.4 copy-done
  92.5 0.4 fusion.19
  92.9 0.9 copy-done.2
  93.8 1.3 fusion.15
  95.4 1.3 convolution_bitcast_fusion.4
  96.7 1.3 convolution_bitcast_fusion.6
  98.0 2.1 fusion.43
  100.1 1.9 add.171
  102.0 2.2 fusion.44
  104.2 1.9 add.173
  106.0 1.3 convolution_bitcast_fusion.2
  107.3 2.2 fusion.45
  109.5 1.9 add.175
  111.4 2.6 %convolution_bitcast_fusion = f32[1024,1,128]{0,2,1:T(8,128)} fusion(bf16[1,8,64,1024]{3,2,1,0:T(8,128)(2,1)} %fusion.15, bf16[128,1,8,128]{0,3,2,1:T(8,128)(2,1)S(1)} %bitcast.467, s32[]{:T(128)S(6)} %select_n.59), kind=kOutput, calls=%fused_computation.52 | convolution fusion | flops 134217728 | bytes 1835012 | tf_op jit(solution)/shard_map/kgrj,rkgd->jkd/dot_general | solution.py:128
  113.9 2.2 fusion.46
  116.1 1.8 add.177
  117.9 2.2 fusion.62
  120.2 2.0 fusion.31
  122.6 1.7 fusion.30
  124.7 1.7 fusion.29
  126.8 1.7 fusion.28
  128.5 1.0 copy-done.10
  129.8 0.9 broadcast_in_dim.109
  131.0 0.9 copy-done.20
  132.1 0.8 copy-done.21
  133.2 0.8 copy-done.22
  134.2 2.5 %convert_element_type.119 = bf16[8192,1,256]{0,2,1:T(8,128)(2,1)} convert(f32[8192,1,256]{0,2,1:T(8,128)S(1)} %fusion.53) | non-fusion elementwise | flops 2097152 | bytes 12582912 | tf_op jit(solution)/shard_map/convert_element_type | solution.py:146
  136.8 0.9 copy-done.16
  138.4 0.7 copy.103
  139.4 0.9 copy.101
  140.5 1.6 fusion.42
  142.1 1.9 add.178
  144.0 1.5 fusion.40
  145.5 1.9 add.180
  147.4 1.5 fusion.39
  148.9 1.8 add.182
  150.7 75.2 %reduce-scatter.2.cloned.1.call-done = bf16[256,1,256]{0,2,1:T(8,128)(2,1)} async-done(((bf16[8192,1,256]{0,2,1:T(8,128)(2,1)}), bf16[256,1,256]{0,2,1:T(8,128)(2,1)}) %reduce-scatter.2.cloned.1.call-update) | async-done | bytes 131088 | tf_op jit(solution)/shard_map/reduce_scatter | solution.py:145
  225.8 0.5 broadcast.172
  226.3 1.6 reduce.11
  228.0 0.7 reshape.512
  228.7 7.0 %all-to-all-start.1 = ((bf16[8,2,4096]{2,1,0:T(2,128)(2,1)}), bf16[8,2,4096]{2,1,0:T(2,128)(2,1)S(1)}, u32[]{:S(2)}, u32[]{:S(2)}) async-start(bf16[8,2,4096]{2,1,0:T(2,128)(2,1)} %reshape.512), calls=%async_computation.2 | async-start | bytes 262144 | tf_op jit(solution)/shard_map/all_to_all | solution.py:148
  235.7 1.5 fusion.38
  237.2 0.3 add.184
  237.8 0.9 copy.102
  238.7 6.1 %all-to-all-done.1 = bf16[8,2,4096]{2,1,0:T(2,128)(2,1)S(1)} async-done(((bf16[8,2,4096]{2,1,0:T(2,128)(2,1)}), bf16[8,2,4096]{2,1,0:T(2,128)(2,1)S(1)}, u32[]{:S(2)}, u32[]{:S(2)}) %all-to-all-start.1) | async-done | bytes 131104 | tf_op jit(solution)/shard_map/all_to_all | solution.py:148
  245.0 0.9 copy.104
  (124 shorter events, 7.9 us)
Async XLA Ops:
  7.2 35.2 %copy-start.34 = (s32[1,128]{1,0:T(1,128)S(1)}, s32[1,128]{1,0:T(1,128)}, u32[]{:S(2)}) copy-start(s32[1,128]{1,0:T(1,128)} %param.10) | copy-start | bytes 1540
  7.2 32.5 %copy-start.29 = (bf16[128,1024]{1,0:T(8,128)(2,1)S(1)}, bf16[128,1024]{1,0:T(8,128)(2,1)}, u32[]{:S(2)}) copy-start(bf16[128,1024]{1,0:T(8,128)(2,1)} %param.6) | copy-start | bytes 786436
  7.2 36.4 %copy-start.31 = (bf16[128,1,256]{2,0,1:T(8,128)(2,1)S(1)}, bf16[128,1,256]{2,0,1:T(8,128)(2,1)}, u32[]{:S(2)}) copy-start(bf16[128,1,256]{2,0,1:T(8,128)(2,1)} %param.7) | copy-start | bytes 196612
  7.2 65.8 %all-gather.2.cloned.1.call-start = ((), (), s32[]{:S(2)}) async-start(), calls=%async_computation.3 | async-start | bytes 4325376 | tf_op jit(solution)/shard_map/all_gather | solution.py:141
  25.7 200.1 %reduce-scatter.2.cloned.1.call-start = ((), (), s32[]{:S(2)}) async-start(), calls=%async_computation.4 | async-start | bytes 4325376 | tf_op jit(solution)/shard_map/reduce_scatter | solution.py:145
  39.6 33.3 %copy-start.17 = (bf16[128,1024]{0,1:T(8,128)(2,1)}, bf16[128,1024]{0,1:T(8,128)(2,1)S(1)}, u32[]{:S(2)}) copy-start(bf16[128,1024]{0,1:T(8,128)(2,1)S(1)} %copy.113) | copy-start | bytes 786436
  43.4 34.0 %copy-start.25 = (bf16[64,1,8,128]{3,2,0,1:T(8,128)(2,1)}, bf16[64,1,8,128]{3,2,0,1:T(8,128)(2,1)S(1)}, u32[]{:S(2)}) copy-start(bf16[64,1,8,128]{3,2,0,1:T(8,128)(2,1)S(1)} %get-tuple-element.23) | copy-start | bytes 393220
  43.5 34.1 %copy-start.23 = (bf16[64,1,8,128]{3,2,0,1:T(8,128)(2,1)}, bf16[64,1,8,128]{3,2,0,1:T(8,128)(2,1)S(1)}, u32[]{:S(2)}) copy-start(bf16[64,1,8,128]{3,2,0,1:T(8,128)(2,1)S(1)} %get-tuple-element.24) | copy-start | bytes 393220
  43.5 37.1 %copy-start.27 = (bf16[64,1,8,128]{3,2,0,1:T(8,128)(2,1)}, bf16[64,1,8,128]{3,2,0,1:T(8,128)(2,1)S(1)}, u32[]{:S(2)}) copy-start(bf16[64,1,8,128]{3,2,0,1:T(8,128)(2,1)S(1)} %get-tuple-element.25) | copy-start | bytes 393220
  90.1 1.7 copy-start.1
  90.2 4.9 %copy-start.15 = (bf16[1,8,128,128]{2,3,1,0:T(8,128)(2,1)}, bf16[1,8,128,128]{2,3,1,0:T(8,128)(2,1)S(1)}, u32[]{:S(2)}) copy-start(bf16[1,8,128,128]{2,3,1,0:T(8,128)(2,1)S(1)} %exponential_convert_fusion) | copy-start | bytes 786436
  90.6 1.9 copy-start
  92.1 1.7 copy-start.2
  92.9 2.3 copy-start.32
  95.4 4.7 %copy-start.14 = (f32[8,128,128]{2,1,0:T(8,128)}, f32[8,128,128]{2,1,0:T(8,128)S(1)}, u32[]{:S(2)}) copy-start(f32[8,128,128]{2,1,0:T(8,128)S(1)} %fusion.72) | copy-start | bytes 1572868
  111.3 2.6 %copy-start.3 = (bf16[1,8,64,1024]{3,2,1,0:T(8,128)(2,1)S(1)}, bf16[1,8,64,1024]{3,2,1,0:T(8,128)(2,1)}, u32[]{:S(2)}) copy-start(bf16[1,8,64,1024]{3,2,1,0:T(8,128)(2,1)} %fusion.15) | copy-start | bytes 3145732
  117.9 4.3 %copy-start.28 = (bf16[64,1,8,128]{3,2,0,1:T(8,128)(2,1)S(1)}, bf16[64,1,8,128]{3,2,0,1:T(8,128)(2,1)}, u32[]{:S(2)}) copy-start(bf16[64,1,8,128]{3,2,0,1:T(8,128)(2,1)} %copy-done.27) | copy-start | bytes 393220
  122.2 2.1 copy-start.4
  122.2 2.1 copy-start.26
  124.3 2.1 copy-start.6
  124.3 2.1 copy-start.24
  126.4 2.0 copy-start.8
  128.5 1.0 copy-start.10
  129.8 1.0 copy-start.19
  130.9 1.0 copy-start.20
  131.9 1.0 copy-start.21
  133.0 1.0 copy-start.22
  136.7 0.9 copy-start.16
  136.8 1.2 copy-start.33
  136.8 1.4 copy-start.18
  136.8 2.4 copy-start.30
  136.8 3.7 %copy-start.11 = (bf16[8,64,1024]{2,1,0:T(8,128)(2,1)S(1)}, bf16[8,64,1024]{2,1,0:T(8,128)(2,1)}, u32[]{:S(2)}) copy-start(bf16[8,64,1024]{2,1,0:T(8,128)(2,1)} %copy-done.10) | copy-start | bytes 3145732
  139.2 4.8 %copy-start.9 = (bf16[8,64,1024]{2,1,0:T(8,128)(2,1)S(1)}, bf16[8,64,1024]{2,1,0:T(8,128)(2,1)}, u32[]{:S(2)}) copy-start(bf16[8,64,1024]{2,1,0:T(8,128)(2,1)} %copy-done.8) | copy-start | bytes 3145732
  140.5 1.6 copy-start.12
  140.5 6.9 %copy-start.7 = (bf16[8,64,1024]{2,1,0:T(8,128)(2,1)S(1)}, bf16[8,64,1024]{2,1,0:T(8,128)(2,1)}, u32[]{:S(2)}) copy-start(bf16[8,64,1024]{2,1,0:T(8,128)(2,1)} %copy-done.6) | copy-start | bytes 3145732
  145.5 90.3 %copy-start.5 = (bf16[8,64,1024]{2,1,0:T(8,128)(2,1)S(1)}, bf16[8,64,1024]{2,1,0:T(8,128)(2,1)}, u32[]{:S(2)}) copy-start(bf16[8,64,1024]{2,1,0:T(8,128)(2,1)} %copy-done.4) | copy-start | bytes 3145732
  150.6 86.6 %copy-start.13 = (f32[128,1,8,128]{3,0,2,1:T(8,128)S(1)}, f32[128,1,8,128]{3,0,2,1:T(8,128)}, u32[]{:S(2)}) copy-start(f32[128,1,8,128]{3,0,2,1:T(8,128)} %add.182) | copy-start | bytes 1572868
  228.7 16.1 %all-to-all-start.1 = ((bf16[8,2,4096]{2,1,0:T(2,128)(2,1)}), bf16[8,2,4096]{2,1,0:T(2,128)(2,1)S(1)}, u32[]{:S(2)}, u32[]{:S(2)}) async-start(bf16[8,2,4096]{2,1,0:T(2,128)(2,1)} %reshape.512), calls=%async_computation.2 | async-start | bytes 262144 | tf_op jit(solution)/shard_map/all_to_all | solution.py:148
Sparse Core Ops, SparseCore 0:
  25.8 47.0 all-gather.1
  136.9 88.8 reduce-scatter.1
where the time goes:
time: 254 us; the launch traced here: 253 us
  waiting for transfers between devices  111 us (44%)
  matrix products  40.7 us (16%)
  local copies, waits for them, and re-layouts  35.5 us (14%)
  between operations  25.2 us (10%)
  blocking collectives  17.5 us (7%)
  other arithmetic  16.2 us (6%)
  starting transfers between devices  7.1 us (3%)
    reduce_scatter x1, waiting for transfers between devices, local(): lax.psum_scatter(prompt_grad.astype(jnp.bfloat16), 'dp', scatter_dimensio...  75.2 us
    all_gather x1, waiting for transfers between devices, local(): whole_prompt = lax.all_gather(regrouped, 'dp', axis=0, tiled=True)  29.1 us
    all_to_all x1, blocking collectives, local(): lax.all_to_all(prompt_kv, 'tensor', split_axis=1, concat_axis=0, tiled=True)  17.5 us
    unnamed x79, local copies, waits for them, and re-layouts  12.3 us
    dot_general x4, matrix products, block_attention(): jnp.einsum('rkgd,jkd->kgrj', q_window, piece[..., :head_width], preferred...  9.75 us
    dot_general x4, matrix products, block_attention(): jnp.einsum('kgrj,jkd->kgrd', probs_now, piece[..., head_width:], preferre...  8.64 us
    add x4, local copies, waits for them, and re-layouts, block_attention(): out + lax.dynamic_update_slice_in_dim(jnp.zeros_like(out), out_window, st...  7.45 us
    dot_general x4, matrix products, block_attention(): jnp.einsum('rkgd,jkd->kgrj', g_window, piece[..., head_width:], preferred...  7.18 us
  transfers between devices with their start and end apart: 3, of which 3 were waited for; matrix products, arithmetic and copies ran while one was open for 9% of the time, Pallas kernels for 0%

commit v1 on v0

v1 whole, which is shorter than its diff:
```python
import math

import jax
import jax.numpy as jnp
from jax import lax
from jax.experimental import pallas as pl
from jax.experimental.pallas import tpu as pltpu
from jax.sharding import PartitionSpec as P

MESH = pl.DeviceIdType.MESH
HD = 128
NH = 8
ROWS = 128
WIN = 64
RESP = 4
WL = NH * WIN
NCH = 4
CK = 256
BLK = 64
SLAB = 32
OFFS = (0, 1, 7, 2, 6, 3, 5, 4)
SCALE = 1.0 / math.sqrt(HD)
ALPHA = SCALE * math.log2(math.e)
BF = jnp.bfloat16
F32 = jnp.float32


def dot(a, b):
    return jnp.dot(a, b, preferred_element_type=F32)


def dot_t(a, b):
    return lax.dot_general(a, b, (((1,), (1,)), ((), ())), preferred_element_type=F32)


class Work:
    def __init__(self, **refs):
        self.__dict__.update(refs)

    def prep(self):
        seg = self.seg[...].astype(F32)
        pos = lax.broadcasted_iota(jnp.int32, (1, ROWS), 1).astype(F32)
        for i in range(1, RESP):
            start = jnp.sum(jnp.where(seg < i, 1.0, 0.0), axis=1, keepdims=True)
            before = jnp.sum(jnp.where(seg < i - 1, 1.0, 0.0), axis=1, keepdims=True)
            pos = pos - jnp.where(seg >= i, start - before, 0.0)
        slot = seg * WIN + pos
        col = seg * (2 * WIN) + pos
        place = lax.broadcasted_iota(jnp.int32, (RESP * WIN, ROWS), 0).astype(F32)
        gather = jnp.where(place == slot, 1.0, 0.0).astype(BF)
        self.kvself[...] = dot(gather, self.rkv[...]).astype(BF)
        slot_t = jnp.broadcast_to(slot, (ROWS, ROWS)).T
        col_t = jnp.broadcast_to(col, (ROWS, ROWS)).T
        lane = lax.broadcasted_iota(jnp.int32, (ROWS, ROWS), 1).astype(F32)
        for i in range(RESP):
            here = lane + 128.0 * i
            self.spread[0:ROWS, i * 128 : (i + 1) * 128] = jnp.where(here == col_t, 1.0, 0.0).astype(BF)
            self.spread[ROWS : 2 * ROWS, i * 128 : (i + 1) * 128] = jnp.where(
                here == col_t + WIN, 1.0, 0.0
            ).astype(BF)
        for i in range(2):
            self.back[:, i * 128 : (i + 1) * 128] = jnp.where(lane + 128.0 * i == slot_t, 1.0, 0.0).astype(BF)
        spread = self.spread[...]
        for source, target in ((self.q, self.qt), (self.g, self.gt)):
            for pair in range(NH // 2):
                two = source[:, pair * 256 : (pair + 1) * 256]
                turned = jnp.concatenate([two[:, :HD].T, two[:, HD:].T], axis=1)
                placed = dot(turned, spread).astype(BF)
                for i in range(RESP):
                    target[i, :, pair * 128 : (pair + 1) * 128] = placed[:, i * 128 : (i + 1) * 128]

    def self_fwd(self):
        key = lax.broadcasted_iota(jnp.int32, (WIN, WL), 0)
        row = lax.broadcasted_iota(jnp.int32, (WIN, WL), 1) & (WIN - 1)
        seen = key <= row

        def body(i, carry):
            kv = self.kvself[pl.ds(pl.multiple_of(i * WIN, WIN), WIN), :]
            s = jnp.where(seen, dot(kv[:, :HD], self.qt[i]), -1e30)
            m = jnp.max(s, axis=0, keepdims=True)
            e = jnp.exp2((s - m) * ALPHA)
            eb = e.astype(BF)
            self.eself[i] = eb
            self.mself[i] = m
            self.accm[i] = m
            self.accl[i] = jnp.sum(e, axis=0, keepdims=True)
            self.acco[i] = dot(kv[:, HD:].T, eb)
            return carry

        lax.fori_loop(0, RESP, body, 0)

    def piece(self, j, i):
        p = self.rp[0, i]
        kv = self.kvb[j][lax.shift_right_logical(p, 1), pl.ds((p & 1) * 2, 2)]
        return kv.reshape(CK, 2 * HD)

    def fwd(self, j):
        def body(i, carry):
            kv = self.piece(j, i)
            s = dot(kv[:, :HD], self.qt[i])
            m = jnp.max(s, axis=0, keepdims=True)
            e = jnp.exp2((s - m) * ALPHA)
            eb = e.astype(BF)
            self.ebuf[j, i] = eb
            self.mbuf[j, i] = m
            total = jnp.sum(e, axis=0, keepdims=True)
            o = dot(kv[:, HD:].T, eb)
            old = self.accm[i]
            new = jnp.maximum(old, m)
            a = jnp.exp2((old - new) * ALPHA)
            b = jnp.exp2((m - new) * ALPHA)
            self.accm[i] = new
            self.accl[i] = self.accl[i] * a + total * b
            self.acco[i] = self.acco[i] * a + o * b
            return carry

        lax.fori_loop(0, RESP, body, 0)

    def middle(self):
        def body(i, carry):
            total = self.accl[i]
            self.lse[i] = self.accm[i] * ALPHA + jnp.log2(total)
            out = self.acco[i] * (1.0 / total)
            self.delta[i] = jnp.sum(self.gt[i].astype(F32) * out, axis=0, keepdims=True)
            self.outt[i] = out.astype(BF)
            return carry

        lax.fori_loop(0, RESP, body, 0)

    def grads(self, i, k, v, m, e):
        weight = e.astype(F32) * jnp.exp2(m * ALPHA - self.lse[i])
        wb = weight.astype(BF)
        ds = (weight * (dot(v, self.gt[i]) - self.delta[i])).astype(BF)
        dk = dot_t(ds, self.qt[i]) * SCALE
        dv = dot_t(wb, self.gt[i])
        dq = dot(k.T, ds)
        return jnp.concatenate([dk, dv], axis=1).astype(BF), dq

    def self_bwd(self):
        def body(i, carry):
            at = pl.ds(pl.multiple_of(i * WIN, WIN), WIN)
            kv = self.kvself[at, :]
            dkv, dq = self.grads(i, kv[:, :HD], kv[:, HD:], self.mself[i], self.eself[i])
            self.dself[at, :] = dkv
            self.dqt[i] = self.dqt[i] + dq
            return carry

        lax.fori_loop(0, RESP, body, 0)

    def bwd(self, j):
        def body(i, carry):
            kv = self.piece(j, i)
            dkv, dq = self.grads(i, kv[:, :HD], kv[:, HD:], self.mbuf[j, i], self.ebuf[j, i])
            self.dkv[j][i] = dkv.reshape(4, BLK, 2 * HD)
            if j == 0:
                self.dqt[i] = dq
            else:
                self.dqt[i] = self.dqt[i] + dq
            return carry

        lax.fori_loop(0, RESP, body, 0)

    def place_rows(self, source, scale, target):
        for head in range(NH):
            at = pl.ds((head // 2) * 128, 128)
            parts = [source[i, :, at] for i in range(RESP)]
            if scale is not None:
                parts = [part * scale for part in parts]
            whole = jnp.concatenate([part.astype(BF) for part in parts], axis=1)
            rows = self.spread[(head % 2) * ROWS : (head % 2 + 1) * ROWS, :]
            target[:, head * HD : (head + 1) * HD] = dot_t(rows, whole).astype(BF)

    def write_attended(self):
        self.place_rows(self.outt, None, self.attended)

    def write_query_grad(self):
        self.place_rows(self.dqt, SCALE, self.qgrad)

    def write_resp_grad(self):
        self.rgrad[...] = dot(self.back[...], self.dself[...]).astype(BF)

    def selected(self, j, p, part):
        total = None
        for i in range(RESP):
            mine = jnp.where(self.rp[0, i] == p, 1.0, 0.0)
            term = self.dkv[j][i, part].astype(F32) * mine
            total = term if total is None else total + term
        return total


WORK_SCRATCH = dict(
    kvself=pltpu.VMEM((RESP * WIN, 2 * HD), BF),
    spread=pltpu.VMEM((2 * ROWS, RESP * 128), BF),
    back=pltpu.VMEM((ROWS, RESP * WIN), BF),
    qt=pltpu.VMEM((RESP, HD, WL), BF),
    gt=pltpu.VMEM((RESP, HD, WL), BF),
    eself=pltpu.VMEM((RESP, WIN, WL), BF),
    ebuf=pltpu.VMEM((NCH, RESP, CK, WL), BF),
    mself=pltpu.VMEM((RESP, 1, WL), F32),
    mbuf=pltpu.VMEM((NCH, RESP, 1, WL), F32),
    accm=pltpu.VMEM((RESP, 1, WL), F32),
    accl=pltpu.VMEM((RESP, 1, WL), F32),
    lse=pltpu.VMEM((RESP, 1, WL), F32),
    delta=pltpu.VMEM((RESP, 1, WL), F32),
    acco=pltpu.VMEM((RESP, HD, WL), F32),
    outt=pltpu.VMEM((RESP, HD, WL), BF),
    dqt=pltpu.VMEM((RESP, HD, WL), F32),
    dself=pltpu.VMEM((RESP * WIN, 2 * HD), BF),
)


class Net:
    def __init__(self, send_sem, recv_sem):
        self.dp, self.t = lax.axis_index("dp"), lax.axis_index("tensor")
        self.x, self.y, self.c = self.dp // 8, (self.dp // 2) % 4, self.dp % 2
        self.send_sem, self.recv_sem = send_sem, recv_sem
        self.count = 0
        self.sent = []

    def device(self, x=None, y=None, c=None, t=None):
        x = self.x if x is None else x
        y = self.y if y is None else y
        c = self.c if c is None else c
        return (x * 8 + y * 2 + c, self.t if t is None else t)

    def along(self, axis, step):
        here = self.x if axis == "x" else self.y
        return self.device(**{axis: (here + step + 4) % 4})

    def copy(self, src, dst, device):
        index = self.count
        self.count += 1
        made = pltpu.make_async_remote_copy(
            src_ref=src,
            dst_ref=dst,
            send_sem=self.send_sem.at[index],
            recv_sem=self.recv_sem.at[index],
            device_id=device,
            device_id_type=MESH,
        )
        made.start()
        self.sent.append(made)
        return made

    def greet(self):
        barrier = pltpu.get_barrier_semaphore()
        partners = [self.along(axis, step) for axis in "xy" for step in (1, 3)]
        partners.append(self.device(c=1 - self.c))
        partners.extend(self.device(t=(self.t + step) % 8) for step in range(1, 8))
        for partner in partners:
            pl.semaphore_signal(barrier, inc=1, device_id=partner, device_id_type=MESH)
        pl.semaphore_wait(barrier, len(partners))

    def finish(self):
        for made in self.sent:
            made.wait_send()


class Gather:
    def __init__(self, net, j, buf):
        self.net, self.j, self.buf = net, j, buf

    def block(self, half, axis, at, first, size):
        rows = pl.ds(half * SLAB + first, size)
        net = self.net
        if axis == "x":
            return self.buf.at[at, slice(None), net.c, rows]
        return self.buf.at[slice(None), at, net.c, rows]

    def own(self, half, x, y, first, size):
        return self.buf.at[x, y, self.net.c, pl.ds(half * SLAB + first, size)]

    def start(self, arrived):
        net = self.net
        self.first = []
        for half in (0, 1):
            if arrived[half] is not None:
                arrived[half].wait_recv()
            axis = "xy"[half]
            mine = self.own(half, net.x, net.y, 0, SLAB)
            self.first.append([net.copy(mine, mine, net.along(axis, step)) for step in (1, 3)])

    def second(self):
        net = self.net
        self.onward = []
        for half in (0, 1):
            axis = "xy"[half]
            here = net.x if axis == "x" else net.y
            copies = []
            for way, step in enumerate((1, 3)):
                self.first[half][way].wait_recv()
                source = (here - step + 4) % 4
                x, y = (source, net.y) if axis == "x" else (net.x, source)
                part = self.own(half, x, y, way * (SLAB // 2), SLAB // 2)
                copies.append(net.copy(part, part, net.along(axis, step)))
            self.onward.append(copies)

    def third(self):
        net = self.net
        self.lines = []
        for half in (0, 1):
            for made in self.onward[half]:
                made.wait_recv()
            axis = "yx"[half]
            here = net.x if axis == "x" else net.y
            line = self.block(half, axis, here, 0, SLAB)
            self.lines.append([net.copy(line, line, net.along(axis, step)) for step in (1, 3)])

    def fourth(self):
        net = self.net
        self.last = []
        for half in (0, 1):
            axis = "yx"[half]
            here = net.x if axis == "x" else net.y
            for way, step in enumerate((1, 3)):
                self.lines[half][way].wait_recv()
                source = (here - step + 4) % 4
                part = self.block(half, axis, source, way * (SLAB // 2), SLAB // 2)
                self.last.append(net.copy(part, part, net.along(axis, step)))

    def across(self):
        net = self.net
        for made in self.last:
            made.wait_recv()
        mine = self.buf.at[:, :, net.c]
        self.sibling = net.copy(mine, mine, net.device(c=1 - net.c))

    def done(self):
        self.sibling.wait_recv()


class Scatter:
    def __init__(self, net, work, j, refs, out):
        self.net, self.work, self.j, self.out = net, work, j, out
        self.__dict__.update(refs)

    def start(self):
        net = self.net

        def body(p, carry):
            for half in (0, 1):
                value = self.work.selected(self.j, p, 2 * half + (1 - net.c))
                self.give[p // 2, (p % 2) * 2 + half] = value.astype(BF)
            return carry

        lax.fori_loop(0, 8, body, 0)
        self.sibling = net.copy(self.give, self.take, net.device(c=1 - net.c))

    def own(self):
        net = self.net
        self.sibling.wait_recv()

        def body(p, carry):
            for half in (0, 1):
                x, y = p // 2, (p % 2) * 2 + half
                value = self.work.selected(self.j, p, 2 * half + net.c) + self.take[x, y].astype(F32)
                self.held[x, y] = value.astype(BF)
            return carry

        lax.fori_loop(0, 8, body, 0)
        self.far = []
        for half in (0, 1):
            axis = "yx"[half]
            here = net.x if axis == "x" else net.y
            across = (here + 2) % 4
            copies = []
            for way, step in enumerate((1, 3)):
                rows = pl.ds(half * SLAB + way * (SLAB // 2), SLAB // 2)
                src = self.held.at[across, :, rows] if axis == "x" else self.held.at[:, across, rows]
                copies.append(net.copy(src, self.far1.at[half, way], net.along(axis, step)))
            self.far.append(copies)

    def line(self, half, axis, at):
        rows = pl.ds(half * SLAB, SLAB)
        return self.held[at, :, rows] if axis == "x" else self.held[:, at, rows]

    def near(self):
        net = self.net
        self.close = []
        for half in (0, 1):
            axis = "yx"[half]
            here = net.x if axis == "x" else net.y
            copies = []
            for way, step in enumerate((1, 3)):
                self.far[half][way].wait_recv()
                mine = self.line(half, axis, (here + step) % 4).astype(F32)
                more = self.far1[half, way].astype(F32)
                part = slice(way * (SLAB // 2), (way + 1) * (SLAB // 2))
                rest = slice((1 - way) * (SLAB // 2), (2 - way) * (SLAB // 2))
                self.near1[half, way, :, part] = (mine[:, part] + more).astype(BF)
                self.near1[half, way, :, rest] = mine[:, rest].astype(BF)
                copies.append(net.copy(self.near1.at[half, way], self.near2.at[half, way], net.along(axis, step)))
            self.close.append(copies)

    def turn(self):
        net = self.net
        self.far = []
        for half in (0, 1):
            axis = "yx"[half]
            here = net.x if axis == "x" else net.y
            total = self.line(half, axis, here).astype(F32)
            for way in (0, 1):
                self.close[half][way].wait_recv()
                total = total + self.near2[half, way].astype(F32)
            self.rest[half] = total.astype(BF)
            axis = "xy"[half]
            here = net.x if axis == "x" else net.y
            copies = []
            for way, step in enumerate((1, 3)):
                src = self.rest.at[half, (here + 2) % 4, pl.ds(way * (SLAB // 2), SLAB // 2)]
                copies.append(net.copy(src, self.far2.at[half, way], net.along(axis, step)))
            self.far.append(copies)

    def near_again(self):
        net = self.net
        self.close = []
        for half in (0, 1):
            axis = "xy"[half]
            here = net.x if axis == "x" else net.y
            copies = []
            for way, step in enumerate((1, 3)):
                self.far[half][way].wait_recv()
                mine = self.rest[half, (here + step) % 4].astype(F32)
                more = self.far2[half, way].astype(F32)
                part = slice(way * (SLAB // 2), (way + 1) * (SLAB // 2))
                rest = slice((1 - way) * (SLAB // 2), (2 - way) * (SLAB // 2))
                self.near3[half, way, part] = (mine[part] + more).astype(BF)
                self.near3[half, way, rest] = mine[rest].astype(BF)
                copies.append(net.copy(self.near3.at[half, way], self.near4.at[half, way], net.along(axis, step)))
            self.close.append(copies)

    def home(self):
        net = self.net
        self.back = []
        for half in (0, 1):
            axis = "xy"[half]
            here = net.x if axis == "x" else net.y
            total = self.rest[half, here].astype(F32)
            for way in (0, 1):
                self.close[half][way].wait_recv()
                total = total + self.near4[half, way].astype(F32)
            away = OFFS[2 * self.j + half]
            if away == 0:
                self.out[net.t] = total.astype(BF)
            else:
                self.ready[half] = total.astype(BF)
                self.back.append(
                    net.copy(self.ready.at[half], self.out.at[net.t], net.device(t=(net.t + away) % 8))
                )

    def done(self):
        for made in self.back:
            made.wait_recv()


SCATTER_SCRATCH = dict(
    give=pltpu.VMEM((4, 4, BLK, 2 * HD), BF),
    take=pltpu.VMEM((4, 4, BLK, 2 * HD), BF),
    held=pltpu.VMEM((4, 4, BLK, 2 * HD), BF),
    far1=pltpu.VMEM((2, 2, 4, SLAB // 2, 2 * HD), BF),
    near1=pltpu.VMEM((2, 2, 4, SLAB, 2 * HD), BF),
    near2=pltpu.VMEM((2, 2, 4, SLAB, 2 * HD), BF),
    rest=pltpu.VMEM((2, 4, SLAB, 2 * HD), BF),
    far2=pltpu.VMEM((2, 2, SLAB // 2, 2 * HD), BF),
    near3=pltpu.VMEM((2, 2, SLAB, 2 * HD), BF),
    near4=pltpu.VMEM((2, 2, SLAB, 2 * HD), BF),
    ready=pltpu.VMEM((2, SLAB, 2 * HD), BF),
)
COPIES = 7 + NCH * (4 + 4 + 4 + 4 + 1) + NCH * (1 + 4 + 4 + 4 + 4) + 7
SCRATCH = (
    [("send_sem", pltpu.SemaphoreType.DMA((COPIES,))), ("recv_sem", pltpu.SemaphoreType.DMA((COPIES,)))]
    + [("kvb", pltpu.VMEM((4, 4, 2, BLK, 2 * HD), BF))] * NCH
    + [("dkv", pltpu.VMEM((RESP, 4, BLK, 2 * HD), BF))] * NCH
    + list(WORK_SCRATCH.items())
    + list(SCATTER_SCRATCH.items()) * NCH
)


def kernel(q, g, rkv, slabs, seg, rp, attended, qgrad, rgrad, pgrad, *scratch):
    named = {}
    for (name, _), ref in zip(SCRATCH, scratch):
        named.setdefault(name, []).append(ref)
    refs = {name: named[name][0] for name in WORK_SCRATCH}
    work = Work(
        q=q, g=g, rkv=rkv, seg=seg, rp=rp, kvb=named["kvb"], dkv=named["dkv"],
        attended=attended, qgrad=qgrad, rgrad=rgrad, **refs
    )
    net = Net(named["send_sem"][0], named["recv_sem"][0])
    gathers = [Gather(net, j, named["kvb"][j]) for j in range(NCH)]
    scatters = [
        Scatter(net, work, j, {name: named[name][j] for name in SCATTER_SCRATCH}, pgrad) for j in range(NCH)
    ]
    net.greet()
    arrivals = [None]
    for place in range(1, 8):
        to = (net.t - OFFS[place] + 8) % 8
        target = gathers[place // 2].own(place % 2, net.x, net.y, 0, SLAB)
        arrivals.append(net.copy(slabs.at[to], target, net.device(t=to)))
    gathers[0].buf[net.x, net.y, net.c, 0:SLAB] = slabs[net.t]
    for j in range(NCH):
        gathers[j].start(arrivals[2 * j : 2 * j + 2])
    work.prep()
    for j in range(NCH):
        gathers[j].second()
    work.self_fwd()
    gathers[0].third()
    gathers[1].third()
    gathers[0].fourth()
    gathers[2].third()
    gathers[0].across()
    gathers[1].fourth()
    gathers[3].third()
    gathers[0].done()
    work.fwd(0)
    gathers[1].across()
    gathers[2].fourth()
    gathers[1].done()
    work.fwd(1)
    gathers[2].across()
    gathers[3].fourth()
    gathers[2].done()
    work.fwd(2)
    gathers[3].across()
    gathers[3].done()
    work.fwd(3)
    work.middle()
    stages = ("start", "own", "near", "turn", "near_again", "home")
    for turn in range(NCH + len(stages) - 1):
        if turn < NCH:
            work.bwd(turn)
        for late in range(len(stages) - 1, -1, -1):
            if 0 <= turn - late < NCH:
                getattr(scatters[turn - late], stages[late])()
        if turn == NCH:
            work.write_attended()
        if turn == NCH + 1:
            work.self_bwd()
            work.write_resp_grad()
        if turn == NCH + 2:
            work.write_query_grad()
    for scatter in scatters:
        scatter.done()
    net.finish()


def local(queries, resp_kv, prompt_kv, resp_prompt, row_segment, cotangent):
    vmem = pl.BlockSpec(memory_space=pltpu.VMEM)
    slabs = prompt_kv.transpose(1, 0, 2)
    attended, query_grad, resp_grad, prompt_grad = pl.pallas_call(
        kernel,
        out_shape=(
            jax.ShapeDtypeStruct((ROWS, NH * HD), BF),
            jax.ShapeDtypeStruct((ROWS, NH * HD), BF),
            jax.ShapeDtypeStruct((ROWS, 2 * HD), BF),
            jax.ShapeDtypeStruct((8, SLAB, 2 * HD), BF),
        ),
        in_specs=[vmem] * 5 + [pl.BlockSpec(memory_space=pltpu.SMEM)],
        out_specs=[vmem] * 4,
        scratch_shapes=[shape for _, shape in SCRATCH],
        compiler_params=pltpu.CompilerParams(
            collective_id=0, has_side_effects=True, vmem_limit_bytes=56 << 20
        ),
    )(queries, cotangent, resp_kv[:, 0], slabs, row_segment, resp_prompt)
    return attended, query_grad, resp_grad[:, None], prompt_grad.transpose(1, 0, 2).astype(F32)


def solution(mesh):
    return jax.shard_map(
        local,
        mesh=mesh,
        in_specs=(
            P("dp", "tensor"),
            P("dp", "tensor", None),
            P(("dp", "tensor"), None, None),
            P("dp", None),
            P("dp", None),
            P("dp", "tensor"),
        ),
        out_specs=(
            P("dp", "tensor"),
            P("dp", "tensor"),
            P("dp", "tensor", None),
            P(("dp", "tensor"), None, None),
        ),
        check_vma=False,
    )
```

time: 254 us -> 90.7 us (0.36)
  waiting for transfers between devices: 111 us -> 0 us
  Pallas kernels: 0 us -> 83.8 us
  matrix products: 40.7 us -> 0 us
  local copies, waits for them, and re-layouts: 35.5 us -> 5.06 us
  between operations: 25.2 us -> 0.65 us
  blocking collectives: 17.5 us -> 0 us
  other arithmetic: 16.2 us -> 0.92 us
  starting transfers between devices: 7.1 us -> 0 us
    pallas_call x0 -> x1, Pallas kernels: none -> 83.8 us  [local(): pl.pallas_call(kernel, out_shape=(jax.ShapeDtypeStruct((ROWS, NH * HD), B...]
    reduce_scatter x1 -> x0, waiting for transfers between devices: 75.2 us -> none  [local(): lax.psum_scatter(prompt_grad.astype(jnp.bfloat16), 'dp', scatter_dimensio...]
    dot_general x30 -> x0, matrix products: 40.7 us -> none  [the longest x4 9.75 us: block_attention(): jnp.einsum('rkgd,jkd->kgrj', q_window, piece[..., :head_width], preferred...]
    all_gather x1 -> x0, waiting for transfers between devices: 29.1 us -> none  [local(): whole_prompt = lax.all_gather(regrouped, 'dp', axis=0, tiled=True)]
    all_to_all x1 -> x0, blocking collectives: 17.5 us -> none  [local(): lax.all_to_all(prompt_kv, 'tensor', split_axis=1, concat_axis=0, tiled=True)]
    add x12 -> x0, local copies, waits for them, and re-layouts: 14.1 us -> none  [the longest x4 7.45 us: block_attention(): out + lax.dynamic_update_slice_in_dim(jnp.zeros_like(out), out_window, st...]
    reduce_sum x5 -> x0, other arithmetic: 8.31 us -> none  [the longest x2 5.28 us: block_attention(): jnp.sum(jnp.exp(prompt_scores[seg] - max_window[..., None]), axis=-1)]
    unnamed x79 -> x11, local copies, waits for them, and re-layouts: 12.3 us -> 5.06 us
  transfers between devices with their start and end apart: 3 -> 0, of which waited for: 3 -> 0; matrix products, arithmetic and copies ran while one was open for 9% -> 0% of each run, Pallas kernels for 0% -> 0%
where the time goes in v1:
time: 90.7 us; the launch traced here: 90.4 us
  Pallas kernels  83.8 us (92%)
  local copies, waits for them, and re-layouts  5.06 us (6%)
  other arithmetic  0.92 us (1%)
    pallas_call x1, Pallas kernels, local(): pl.pallas_call(kernel, out_shape=(jax.ShapeDtypeStruct((ROWS, NH * HD), B...  83.8 us
    unnamed x11, local copies, waits for them, and re-layouts  5.06 us

profile of v1, /device:TPU:2, one launch (start us, length us, event | category | flops | bytes accessed | tf_op | source)
XLA Modules:
  0.0 90.4 jit_solution(10432494312806149908)
XLA Ops:
  0.6 1.6 %copy.13 = bf16[32,8,256]{2,0,1:T(8,128)(2,1)} copy(bf16[32,8,256]{2,1,0:T(8,128)(2,1)} %param.8) | data formatting | bytes 262144 | tf_op args[2]
  2.2 83.8 %shard_map.93 = (bf16[128,1024]{1,0:T(8,128)(2,1)}, bf16[128,1024]{1,0:T(8,128)(2,1)}, bf16[128,256]{1,0:T(8,128)(2,1)}, bf16[8,32,256]{2,1,0:T(8,128)(2,1)}) custom-call(bf16[128,1024]{1,0:T(8,128)(2,1)} %q.1, bf16[128,1024]{1,0:T(8,128)(2,1)} %g.1, bf16[128,256]{1,0:T(8,128)(2,1)} %bitcast.9, bf16[8,32,256]{2,1,0:T(8,128)(2,1)} %bitcast.7, s32[1,128]{1,0:T(1,128)} %seg.1, ...), custom_call_target="tpu_custom_call" | custom-call | tf_op jit(solution)/shard_map/pallas_call | solution.py:549
  86.0 0.9 %convert_bitcast_fusion = f32[32,8,256]{2,0,1:T(8,128)S(1)} fusion(bf16[8,32,256]{2,1,0:T(8,128)(2,1)} %get-tuple-element.11), kind=kLoop, calls=%fused_computation | loop fusion | flops 65536 | bytes 393216 | tf_op jit(solution)/shard_map/convert_element_type | solution.py:564
  86.9 0.0 copy-start.1
  87.0 0.9 copy.11
  87.8 0.1 copy-done.1
  87.9 0.0 copy-start
  87.9 0.7 copy.17
  88.6 0.3 copy-done
  88.9 0.0 copy-start.2
  88.9 0.7 copy.18
  89.6 0.2 copy-done.2
  89.8 0.6 copy.19
Async XLA Ops:
  86.9 1.0 %copy-start.1 = (bf16[128,1024]{1,0:T(8,128)(2,1)S(1)}, bf16[128,1024]{1,0:T(8,128)(2,1)}, u32[]{:S(2)}) copy-start(bf16[128,1024]{1,0:T(8,128)(2,1)} %get-tuple-element.20) | copy-start | bytes 786436
  87.9 1.0 %copy-start = (bf16[128,1024]{1,0:T(8,128)(2,1)S(1)}, bf16[128,1024]{1,0:T(8,128)(2,1)}, u32[]{:S(2)}) copy-start(bf16[128,1024]{1,0:T(8,128)(2,1)} %get-tuple-element.21) | copy-start | bytes 786436
  88.9 0.9 copy-start.2

commit v2 on v1

v2 whole, which is shorter than its diff:
```python
import math

import jax
import jax.numpy as jnp
from jax import lax
from jax.experimental import pallas as pl
from jax.experimental.pallas import tpu as pltpu
from jax.sharding import PartitionSpec as P

MESH = pl.DeviceIdType.MESH
HD = 128
NH = 8
ROWS = 128
WIN = 64
RESP = 4
WL = NH * WIN
NCH = 4
CK = 256
BLK = 64
SLAB = 32
OFFS = (0, 1, 7, 2, 6, 3, 5, 4)
GATHER_MERGED = (1, 2)
GATHER_RELAYED = (0, 1, 2, 3)
SCATTER_RELAYED = ()
SCATTER_MERGED = (1,)
SCALE = 1.0 / math.sqrt(HD)
ALPHA = SCALE * math.log2(math.e)
BF = jnp.bfloat16
F32 = jnp.float32


def dot(a, b):
    return jnp.dot(a, b, preferred_element_type=F32)


def dot_t(a, b):
    return lax.dot_general(a, b, (((1,), (1,)), ((), ())), preferred_element_type=F32)


class Work:
    def __init__(self, **refs):
        self.__dict__.update(refs)

    def prep(self):
        seg = self.seg[...].astype(F32)
        pos = lax.broadcasted_iota(jnp.int32, (1, ROWS), 1).astype(F32)
        for i in range(1, RESP):
            start = jnp.sum(jnp.where(seg < i, 1.0, 0.0), axis=1, keepdims=True)
            before = jnp.sum(jnp.where(seg < i - 1, 1.0, 0.0), axis=1, keepdims=True)
            pos = pos - jnp.where(seg >= i, start - before, 0.0)
        slot = seg * WIN + pos
        col = seg * (2 * WIN) + pos
        place = lax.broadcasted_iota(jnp.int32, (RESP * WIN, ROWS), 0).astype(F32)
        gather = jnp.where(place == slot, 1.0, 0.0).astype(BF)
        self.kvself[...] = dot(gather, self.rkv[...]).astype(BF)
        slot_t = jnp.broadcast_to(slot, (ROWS, ROWS)).T
        col_t = jnp.broadcast_to(col, (ROWS, ROWS)).T
        lane = lax.broadcasted_iota(jnp.int32, (ROWS, ROWS), 1).astype(F32)
        for i in range(RESP):
            here = lane + 128.0 * i
            self.spread[0:ROWS, i * 128 : (i + 1) * 128] = jnp.where(here == col_t, 1.0, 0.0).astype(BF)
            self.spread[ROWS : 2 * ROWS, i * 128 : (i + 1) * 128] = jnp.where(
                here == col_t + WIN, 1.0, 0.0
            ).astype(BF)
        for i in range(2):
            self.back[:, i * 128 : (i + 1) * 128] = jnp.where(lane + 128.0 * i == slot_t, 1.0, 0.0).astype(BF)
        spread = self.spread[...]
        for source, target in ((self.q, self.qt), (self.g, self.gt)):
            for pair in range(NH // 2):
                two = source[:, pair * 256 : (pair + 1) * 256]
                turned = jnp.concatenate([two[:, :HD].T, two[:, HD:].T], axis=1)
                placed = dot(turned, spread).astype(BF)
                for i in range(RESP):
                    target[i, :, pair * 128 : (pair + 1) * 128] = placed[:, i * 128 : (i + 1) * 128]

    def self_fwd(self):
        key = lax.broadcasted_iota(jnp.int32, (WIN, WL), 0)
        row = lax.broadcasted_iota(jnp.int32, (WIN, WL), 1) & (WIN - 1)
        seen = key <= row

        def body(i, carry):
            k = self.kvself[pl.ds(pl.multiple_of(i * WIN, WIN), WIN), 0:HD]
            s = jnp.where(seen, dot(k, self.qt[i]), -1e30)
            m = jnp.max(s, axis=0, keepdims=True)
            e = jnp.exp2((s - m) * ALPHA)
            self.wself[i] = e.astype(BF)
            self.mself[i] = m
            self.accm[i] = m
            self.accl[i] = jnp.sum(e, axis=0, keepdims=True)
            return carry

        lax.fori_loop(0, RESP, body, 0, unroll=True)

    def piece(self, bufs, j, i):
        p = self.rp[0, i]
        return bufs[j][lax.shift_right_logical(p, 1), pl.ds((p & 1) * 2, 2)].reshape(CK, HD)

    def fwd(self, j):
        def body(i, carry):
            s = dot(self.piece(self.kb, j, i), self.qt[i])
            m = jnp.max(s, axis=0, keepdims=True)
            e = jnp.exp2((s - m) * ALPHA)
            self.weight[j, i] = e.astype(BF)
            self.mbuf[j, i] = m
            old = self.accm[i]
            new = jnp.maximum(old, m)
            self.accl[i] = self.accl[i] * jnp.exp2((old - new) * ALPHA) + jnp.sum(
                e, axis=0, keepdims=True
            ) * jnp.exp2((m - new) * ALPHA)
            self.accm[i] = new
            return carry

        lax.fori_loop(0, RESP, body, 0, unroll=True)

    def middle(self):
        def body(i, carry):
            lse = self.accm[i] * ALPHA + jnp.log2(self.accl[i])
            self.lse[i] = lse
            weight = (self.wself[i].astype(F32) * jnp.exp2(self.mself[i] * ALPHA - lse)).astype(BF)
            self.wself[i] = weight
            v = self.kvself[pl.ds(pl.multiple_of(i * WIN, WIN), WIN), HD : 2 * HD]
            self.acco[i] = dot(v.T, weight)
            return carry

        lax.fori_loop(0, RESP, body, 0, unroll=True)

    def gradv(self, j):
        def body(i, carry):
            weight = self.weight[j, i].astype(F32) * jnp.exp2(self.mbuf[j, i] * ALPHA - self.lse[i])
            weight = weight.astype(BF)
            self.weight[j, i] = weight
            self.grads["v"][j][i] = dot_t(weight, self.gt[i]).astype(BF).reshape(4, BLK, HD)
            return carry

        lax.fori_loop(0, RESP, body, 0, unroll=True)

    def out(self, j):
        def body(i, carry):
            self.acco[i] = self.acco[i] + dot(self.piece(self.vb, j, i).T, self.weight[j, i])
            return carry

        lax.fori_loop(0, RESP, body, 0, unroll=True)

    def deltas(self):
        def body(i, carry):
            out = self.acco[i]
            self.delta[i] = jnp.sum(self.gt[i].astype(F32) * out, axis=0, keepdims=True)
            self.outt[i] = out.astype(BF)
            return carry

        lax.fori_loop(0, RESP, body, 0, unroll=True)

    def dscore(self, i, v, weight):
        return (weight.astype(F32) * (dot(v, self.gt[i]) - self.delta[i])).astype(BF)

    def self_bwd(self):
        def body(i, carry):
            at = pl.ds(pl.multiple_of(i * WIN, WIN), WIN)
            kv = self.kvself[at, :]
            ds = self.dscore(i, kv[:, HD:], self.wself[i])
            dk = dot_t(ds, self.qt[i]) * SCALE
            dv = dot_t(self.wself[i], self.gt[i])
            self.dself[at, :] = jnp.concatenate([dk, dv], axis=1).astype(BF)
            self.dqt[i] = dot(kv[:, :HD].T, ds)
            return carry

        lax.fori_loop(0, RESP, body, 0, unroll=True)

    def bwd(self, j):
        def body(i, carry):
            ds = self.dscore(i, self.piece(self.vb, j, i), self.weight[j, i])
            self.grads["k"][j][i] = (dot_t(ds, self.qt[i]) * SCALE).astype(BF).reshape(4, BLK, HD)
            self.weight[j, i] = ds
            return carry

        lax.fori_loop(0, RESP, body, 0, unroll=True)

    def gradq(self):
        def body(i, carry):
            total = self.dqt[i]
            for j in range(NCH):
                total = total + dot(self.piece(self.kb, j, i).T, self.weight[j, i])
            self.dqt[i] = total
            return carry

        lax.fori_loop(0, RESP, body, 0, unroll=True)

    def place_rows(self, source, scale, target):
        for head in range(NH):
            at = pl.ds((head // 2) * 128, 128)
            parts = [source[i, :, at] for i in range(RESP)]
            if scale is not None:
                parts = [part * scale for part in parts]
            whole = jnp.concatenate([part.astype(BF) for part in parts], axis=1)
            rows = self.spread[(head % 2) * ROWS : (head % 2 + 1) * ROWS, :]
            target[:, head * HD : (head + 1) * HD] = dot_t(rows, whole).astype(BF)

    def write_attended(self):
        self.place_rows(self.outt, None, self.attended)

    def write_query_grad(self):
        self.place_rows(self.dqt, SCALE, self.qgrad)

    def write_resp_grad(self):
        self.rgrad[...] = dot(self.back[...], self.dself[...]).astype(BF)

    def selected(self, kind, j, p, part):
        total = None
        for i in range(RESP):
            mine = jnp.where(self.rp[0, i] == p, 1.0, 0.0).astype(BF)
            term = self.grads[kind][j][i, part] * mine
            total = term if total is None else total + term
        return total


WORK_SCRATCH = dict(
    kvself=pltpu.VMEM((RESP * WIN, 2 * HD), BF),
    spread=pltpu.VMEM((2 * ROWS, RESP * 128), BF),
    back=pltpu.VMEM((ROWS, RESP * WIN), BF),
    qt=pltpu.VMEM((RESP, HD, WL), BF),
    gt=pltpu.VMEM((RESP, HD, WL), BF),
    wself=pltpu.VMEM((RESP, WIN, WL), BF),
    weight=pltpu.VMEM((NCH, RESP, CK, WL), BF),
    mself=pltpu.VMEM((RESP, 1, WL), F32),
    mbuf=pltpu.VMEM((NCH, RESP, 1, WL), F32),
    accm=pltpu.VMEM((RESP, 1, WL), F32),
    accl=pltpu.VMEM((RESP, 1, WL), F32),
    lse=pltpu.VMEM((RESP, 1, WL), F32),
    delta=pltpu.VMEM((RESP, 1, WL), F32),
    acco=pltpu.VMEM((RESP, HD, WL), F32),
    outt=pltpu.VMEM((RESP, HD, WL), BF),
    dqt=pltpu.VMEM((RESP, HD, WL), F32),
    dself=pltpu.VMEM((RESP * WIN, 2 * HD), BF),
)


class Net:
    def __init__(self, send_sem, recv_sem):
        self.dp, self.t = lax.axis_index("dp"), lax.axis_index("tensor")
        self.x, self.y, self.c = self.dp // 8, (self.dp // 2) % 4, self.dp % 2
        self.send_sem, self.recv_sem = send_sem, recv_sem
        self.count = 0
        self.sent = []

    def at(self, axis):
        return self.x if axis == "x" else self.y

    def device(self, axis=None, step=0, up=0, other=False):
        x = (self.x + step) % 4 if axis == "x" else self.x
        y = (self.y + step) % 4 if axis == "y" else self.y
        c = 1 - self.c if other else self.c
        return (x * 8 + y * 2 + c, (self.t + up) % 8)

    def copy(self, src, dst, device):
        index = self.count
        self.count += 1
        if index >= SENDS:
            self.sent[index - SENDS].wait_send()
        made = pltpu.make_async_remote_copy(
            src_ref=src,
            dst_ref=dst,
            send_sem=self.send_sem.at[index % SENDS],
            recv_sem=self.recv_sem.at[index],
            device_id=device,
            device_id_type=MESH,
        )
        made.start()
        self.sent.append(made)
        return made

    def greet(self, targets):
        barrier = pltpu.get_barrier_semaphore()
        for axis, step, up, other in targets:
            pl.semaphore_signal(
                barrier, inc=1, device_id=self.device(axis, 4 - step, 8 - up, other), device_id_type=MESH
            )

    def greeted(self, targets):
        pl.semaphore_wait(pltpu.get_barrier_semaphore(), len(targets))

    def finish(self):
        for made in self.sent[-SENDS:]:
            made.wait_send()


def first_axis(place):
    return "xy"[place % 2]


def second_axis(place):
    return "yx"[place % 2]


def targets():
    found = {(None, 0, 0, True)}
    for axis in "xy":
        found.update((axis, step, 0, False) for step in (1, 2, 3))
    for place in range(1, 8):
        for merged, up in ((GATHER_MERGED, -OFFS[place] % 8), (SCATTER_MERGED, OFFS[place])):
            found.add((None, 0, up, False))
            if place in merged:
                found.update((first_axis(place), step, up, False) for step in (1, 2, 3))
    return sorted(found, key=str)


class Gather:
    def __init__(self, net, place, buf):
        self.net, self.place, self.buf = net, place, buf
        self.low = (place % 2) * SLAB

    def line(self, axis, at, low=0, size=SLAB):
        rows = pl.ds(self.low + low, size)
        if axis == "x":
            return self.buf.at[at, :, self.net.c, rows]
        return self.buf.at[:, at, self.net.c, rows]

    def mine(self):
        net = self.net
        return self.buf.at[net.x, net.y, net.c, pl.ds(self.low, SLAB)]

    def up(self, slabs):
        net, place, axis = self.net, self.place, first_axis(self.place)
        away = -OFFS[place] % 8
        slab = slabs.at[(net.t + away) % 8]
        self.arrived, self.lined = None, []
        if place == 0:
            self.buf[net.x, net.y, net.c, 0:SLAB] = slab[...]
            self.lined = [net.copy(slab, self.mine(), net.device(axis, step)) for step in (1, 2, 3)]
        elif place in GATHER_MERGED:
            self.lined = [net.copy(slab, self.mine(), net.device(axis, step, away)) for step in (1, 2, 3, 0)]
        else:
            self.arrived = net.copy(slab, self.mine(), net.device(None, 0, away))

    def first(self):
        if self.arrived is not None:
            net, axis = self.net, first_axis(self.place)
            self.arrived.wait_recv()
            self.lined = [net.copy(self.mine(), self.mine(), net.device(axis, step)) for step in (1, 2, 3)]

    def second(self):
        net, axis = self.net, second_axis(self.place)
        for made in self.lined:
            made.wait_recv()
        whole = self.line(axis, net.at(axis))
        steps = (1, 3) if self.place in GATHER_RELAYED else (1, 2, 3)
        self.lines = [net.copy(whole, whole, net.device(axis, step)) for step in steps]

    def relay(self):
        if self.place in GATHER_RELAYED:
            net, axis = self.net, second_axis(self.place)
            handed = []
            for way, step in enumerate((1, 3)):
                self.lines[way].wait_recv()
                part = self.line(axis, (net.at(axis) + 4 - step) % 4, way * (SLAB // 2), SLAB // 2)
                handed.append(net.copy(part, part, net.device(axis, step)))
            self.lines = handed

    def across(self):
        net = self.net
        for made in self.lines:
            made.wait_recv()
        held = self.buf.at[:, :, net.c, pl.ds(self.low, SLAB)]
        self.sibling = net.copy(held, held, net.device(other=True))

    def done(self):
        self.sibling.wait_recv()


class Scatter:
    def __init__(self, net, work, kind, j, refs, final, heads):
        self.net, self.work, self.kind, self.j, self.final, self.heads = net, work, kind, j, final, heads
        self.relayed = f"{kind}{j}" in SCATTER_RELAYED
        self.__dict__.update(refs)

    def start(self):
        net = self.net

        def body(p, carry):
            for half in (0, 1):
                value = self.work.selected(self.kind, self.j, p, 2 * half + (1 - net.c))
                self.give[p // 2, (p % 2) * 2 + half] = value
            return carry

        lax.fori_loop(0, 8, body, 0, unroll=4)
        self.sibling = net.copy(self.give, self.take, net.device(other=True))

    def line(self, half, axis, at, low=0, size=SLAB):
        rows = pl.ds(half * SLAB + low, size)
        return self.held.at[at, :, rows] if axis == "x" else self.held.at[:, at, rows]

    def own(self):
        net = self.net
        self.sibling.wait_recv()

        def body(p, carry):
            for half in (0, 1):
                x, y = p // 2, (p % 2) * 2 + half
                value = self.work.selected(self.kind, self.j, p, 2 * half + net.c)
                self.held[x, y] = (value.astype(F32) + self.take[x, y].astype(F32)).astype(BF)
            return carry

        lax.fori_loop(0, 8, body, 0, unroll=4)
        self.lined = []
        for half in (0, 1):
            axis = second_axis(half)
            if self.relayed:
                copies = []
                for way, step in enumerate((1, 3)):
                    part = pl.ds(way * (SLAB // 2), SLAB // 2)
                    src = self.line(half, axis, (net.at(axis) + 2) % 4, way * (SLAB // 2), SLAB // 2)
                    copies.append(net.copy(src, self.came.at[half, 2, :, part], net.device(axis, step)))
                self.lined.append(copies)
                continue
            self.lined.append(
                [
                    net.copy(
                        self.line(half, axis, (net.at(axis) + step) % 4),
                        self.came.at[half, step - 1],
                        net.device(axis, step),
                    )
                    for step in (1, 2, 3)
                ]
            )

    def near(self):
        if self.relayed:
            net = self.net
            far, self.lined = self.lined, []
            for half in (0, 1):
                axis = second_axis(half)
                copies = []
                for way, step in enumerate((1, 3)):
                    far[half][way].wait_recv()
                    mine = self.line(half, axis, (net.at(axis) + step) % 4)[...]
                    part = slice(way * (SLAB // 2), (way + 1) * (SLAB // 2))
                    rest = slice((1 - way) * (SLAB // 2), (2 - way) * (SLAB // 2))
                    added = mine[:, part].astype(F32) + self.came[half, 2, :, part].astype(F32)
                    self.handed[half, way, :, part] = added.astype(BF)
                    self.handed[half, way, :, rest] = mine[:, rest]
                    copies.append(
                        net.copy(self.handed.at[half, way], self.came.at[half, way], net.device(axis, step))
                    )
                self.lined.append(copies)

    def turn(self):
        net = self.net
        self.homeward = []
        for half in (0, 1):
            axis = second_axis(half)
            total = self.line(half, axis, net.at(axis))[...].astype(F32)
            for index, made in enumerate(self.lined[half]):
                made.wait_recv()
                total = total + self.came[half, index].astype(F32)
            self.rest[half] = total.astype(BF)
            place, axis = 2 * self.j + half, first_axis(half)
            away = OFFS[place] if place in SCATTER_MERGED else 0
            copies = []
            for step in (1, 2, 3, 0):
                src, dst = self.rest.at[half, (net.at(axis) + step) % 4], self.final.at[place, step]
                if away == 0 and step == 0:
                    self.final[place, 0] = src[...]
                else:
                    copies.append(net.copy(src, dst, net.device(axis, step, away)))
            self.homeward.append(copies)

    def summed(self, place, half):
        for made in self.homeward[half]:
            made.wait_recv()
        total = self.final[place, 0].astype(F32)
        for step in (1, 2, 3):
            total = total + self.final[place, step].astype(F32)
        return total

    def up(self):
        net = self.net
        self.last = [None, None]
        for half in (0, 1):
            place = 2 * self.j + half
            if OFFS[place] != 0 and place not in SCATTER_MERGED:
                self.ready[half] = self.summed(place, half).astype(BF)
                self.last[half] = net.copy(
                    self.ready.at[half], self.came_up.at[half], net.device(None, 0, OFFS[place])
                )

    def sum(self):
        net = self.net
        for half in (0, 1):
            place = 2 * self.j + half
            head = (net.t + 8 - OFFS[place]) % 8
            lanes = slice(0, HD) if self.kind == "k" else slice(HD, 2 * HD)
            if self.last[half] is None:
                self.heads[head, :, lanes] = self.summed(place, half)
            else:
                self.last[half].wait_recv()
                self.heads[head, :, lanes] = self.came_up[half].astype(F32)


SCATTER_SCRATCH = dict(
    give=pltpu.VMEM((4, 4, BLK, HD), BF),
    take=pltpu.VMEM((4, 4, BLK, HD), BF),
    held=pltpu.VMEM((4, 4, BLK, HD), BF),
    came=pltpu.VMEM((2, 3, 4, SLAB, HD), BF),
    handed=pltpu.VMEM((2, 2, 4, SLAB, HD), BF),
    rest=pltpu.VMEM((2, 4, SLAB, HD), BF),
    ready=pltpu.VMEM((2, SLAB, HD), BF),
    came_up=pltpu.VMEM((2, SLAB, HD), BF),
)
COPIES = 252
SENDS = 64
SCRATCH = (
    [("send_sem", pltpu.SemaphoreType.DMA((SENDS,))), ("recv_sem", pltpu.SemaphoreType.DMA((COPIES,)))]
    + [("kb", pltpu.VMEM((4, 4, 2, BLK, HD), BF)), ("vb", pltpu.VMEM((4, 4, 2, BLK, HD), BF))] * NCH
    + [("dk", pltpu.VMEM((RESP, 4, BLK, HD), BF)), ("dv", pltpu.VMEM((RESP, 4, BLK, HD), BF))] * NCH
    + [
        ("kslabs", pltpu.VMEM((8, SLAB, HD), BF)),
        ("vslabs", pltpu.VMEM((8, SLAB, HD), BF)),
        ("wide", pltpu.VMEM((2, SLAB * 8, HD), F32)),
        ("final", pltpu.VMEM((8, 4, SLAB, HD), BF)),
        ("final", pltpu.VMEM((8, 4, SLAB, HD), BF)),
        ("near_sem", pltpu.SemaphoreType.DMA((9,))),
        ("q", pltpu.VMEM((ROWS, NH * HD), BF)),
        ("g", pltpu.VMEM((ROWS, NH * HD), BF)),
        ("rkv", pltpu.VMEM((ROWS, 2 * HD), BF)),
        ("pkv", pltpu.VMEM((SLAB, 8, 2 * HD), BF)),
        ("seg", pltpu.VMEM((1, ROWS), jnp.int32)),
        ("attended", pltpu.VMEM((ROWS, NH * HD), BF)),
        ("qgrad", pltpu.VMEM((ROWS, NH * HD), BF)),
        ("rgrad", pltpu.VMEM((ROWS, 2 * HD), BF)),
        ("heads", pltpu.VMEM((8, SLAB, 2 * HD), F32)),
        ("pgrad", pltpu.VMEM((SLAB, 8, 2 * HD), F32)),
    ]
    + list(WORK_SCRATCH.items())
    + list(SCATTER_SCRATCH.items()) * (2 * NCH)
)


INPUTS = ("pkv", "q", "g", "rkv", "seg")
OUTPUTS = ("attended", "qgrad", "rgrad", "pgrad")


def kernel(q, g, rkv, pkv, seg, rp, attended, qgrad, rgrad, pgrad, *scratch):
    outer = dict(q=q, g=g, rkv=rkv, pkv=pkv, seg=seg, attended=attended, qgrad=qgrad, rgrad=rgrad, pgrad=pgrad)
    named = {}
    for (name, _), ref in zip(SCRATCH, scratch):
        named.setdefault(name, []).append(ref)
    inner = {name: named[name][0] for name in outer}
    refs = {name: named[name][0] for name in WORK_SCRATCH}
    work = Work(rp=rp, kb=named["kb"], vb=named["vb"], grads=dict(k=named["dk"], v=named["dv"]), **inner, **refs)
    near_sem = named["near_sem"][0]
    moves = {}
    for index, name in enumerate(INPUTS):
        moves[name] = pltpu.make_async_copy(outer[name], inner[name], near_sem.at[index])
    for index, name in enumerate(OUTPUTS):
        moves[name] = pltpu.make_async_copy(inner[name], outer[name], near_sem.at[len(INPUTS) + index])
    moves["pkv"].start()
    net = Net(named["send_sem"][0], named["recv_sem"][0])
    slabs = dict(k=named["kslabs"][0], v=named["vslabs"][0])
    wide, heads = named["wide"][0], named["heads"][0]
    gk = [Gather(net, place, named["kb"][place // 2]) for place in range(8)]
    gv = [Gather(net, place, named["vb"][place // 2]) for place in range(8)]
    scatters = []
    for index in range(2 * NCH):
        scratch_of = {name: named[name][index] for name in SCATTER_SCRATCH}
        kind, j = "kv"[index // NCH], index % NCH
        scatters.append(Scatter(net, work, kind, j, scratch_of, named["final"][index // NCH], heads))
    sk, sv = scatters[:NCH], scatters[NCH:]
    net.greet(targets())
    for name in INPUTS[1:]:
        moves[name].start()
    moves["pkv"].wait()
    pkv = inner["pkv"]
    for part in (0, 1):
        wide[part] = pkv[:, :, part * HD : (part + 1) * HD].astype(F32).reshape(SLAB * 8, HD)
    for head in range(8):
        for part in (0, 1):
            slabs["kv"[part]][head] = wide[part, pl.ds(head, SLAB, stride=8), :].astype(BF)
    net.greeted(targets())
    for gather in gk:
        gather.up(slabs["k"])
    for gather in gv:
        gather.up(slabs["v"])
    for name in INPUTS[1:]:
        moves[name].wait()
    work.prep()
    work.self_fwd()
    gk[0].second()
    gv[0].second()
    gk[1].second()
    gk[3].first()
    gk[4].first()
    gk[2].second()
    gk[5].first()
    gk[6].first()
    gv[1].second()
    gv[3].first()
    gv[2].second()
    gv[4].first()
    gk[7].first()
    gk[0].relay()
    gv[5].first()
    gv[6].first()
    gv[0].relay()
    gk[1].relay()
    gv[7].first()
    gk[3].second()
    gk[4].second()
    gk[2].relay()
    gk[6].second()
    gv[1].relay()
    gk[5].second()
    gv[3].second()
    gv[2].relay()
    gv[4].second()
    gk[0].across()
    gk[1].across()
    gk[7].second()
    gv[6].second()
    gv[0].across()
    gv[5].second()
    gk[3].relay()
    gk[0].done()
    gk[1].done()
    work.fwd(0)
    gv[1].across()
    gv[7].second()
    gk[2].across()
    gk[4].across()
    gk[5].across()
    gv[3].relay()
    gv[2].across()
    gk[6].across()
    gk[4].done()
    gk[5].done()
    work.fwd(2)
    gk[7].across()
    gv[4].across()
    gk[3].across()
    gk[6].done()
    gk[7].done()
    work.fwd(3)
    gv[5].across()
    gv[6].across()
    gk[2].done()
    gk[3].done()
    work.fwd(1)
    gv[3].across()
    work.middle()
    gv[7].across()
    work.gradv(3)
    sv[3].start()
    work.gradv(2)
    sv[2].start()
    gv[4].done()
    gv[5].done()
    work.out(2)
    gv[6].done()
    gv[7].done()
    work.out(3)
    work.gradv(1)
    sv[1].start()
    sv[3].own()
    gv[2].done()
    gv[3].done()
    work.out(1)
    sv[2].own()
    work.gradv(0)
    sv[0].start()
    sv[1].own()
    gv[0].done()
    gv[1].done()
    work.out(0)
    work.deltas()
    work.bwd(3)
    sk[3].start()
    sv[0].own()
    work.bwd(2)
    sk[2].start()
    sk[3].own()
    work.bwd(1)
    sk[1].start()
    sk[2].own()
    work.bwd(0)
    sk[0].start()
    sk[1].own()
    sv[3].turn()
    sv[2].turn()
    sv[1].turn()
    sk[0].own()
    sk[3].turn()
    sv[0].turn()
    work.write_attended()
    moves["attended"].start()
    work.self_bwd()
    sk[2].turn()
    work.write_resp_grad()
    moves["rgrad"].start()
    work.gradq()
    work.write_query_grad()
    moves["qgrad"].start()
    sk[1].turn()
    sv[3].up()
    sv[2].up()
    sv[1].up()
    sk[0].turn()
    sk[3].up()
    sk[2].up()
    sv[0].up()
    sv[0].sum()
    sk[1].up()
    sv[1].sum()
    sv[2].sum()
    sv[3].sum()
    sk[0].up()
    sk[0].sum()
    sk[1].sum()
    sk[2].sum()
    sk[3].sum()
    for head in range(8):
        inner["pgrad"][:, head, :] = heads[head]
    moves["pgrad"].start()
    net.finish()
    for name in OUTPUTS:
        moves[name].wait()


def hand_on(*refs):
    sems, held, refs = refs[-1], refs[-5:-1], refs[:-5]
    inward = [pltpu.make_async_copy(refs[i], held[i], sems.at[i]) for i in range(4)]
    outward = [pltpu.make_async_copy(held[i], refs[4 + i], sems.at[4 + i]) for i in range(4)]
    for copy in inward:
        copy.start()
    for before, after in zip(inward, outward):
        before.wait()
        after.start()
    for copy in outward:
        copy.wait()


def local(queries, resp_kv, prompt_kv, resp_prompt, row_segment, cotangent):
    anywhere = pl.BlockSpec(memory_space=pl.ANY)
    shapes = (
        jax.ShapeDtypeStruct((ROWS, NH * HD), BF),
        jax.ShapeDtypeStruct((ROWS, NH * HD), BF),
        jax.ShapeDtypeStruct((ROWS, 2 * HD), BF),
        jax.ShapeDtypeStruct((SLAB, 8, 2 * HD), F32),
    )
    results = pl.pallas_call(
        kernel,
        out_shape=shapes,
        in_specs=[anywhere] * 5 + [pl.BlockSpec(memory_space=pltpu.SMEM)],
        out_specs=[anywhere] * 4,
        scratch_shapes=[shape for _, shape in SCRATCH],
        compiler_params=pltpu.CompilerParams(
            collective_id=0, has_side_effects=True, vmem_limit_bytes=56 << 20
        ),
    )(queries, cotangent, resp_kv[:, 0], prompt_kv, row_segment, resp_prompt)
    attended, query_grad, resp_grad, prompt_grad = pl.pallas_call(
        hand_on,
        out_shape=shapes,
        in_specs=[anywhere] * 4,
        out_specs=[anywhere] * 4,
        scratch_shapes=[pltpu.VMEM(shape.shape, shape.dtype) for shape in shapes] + [pltpu.SemaphoreType.DMA((8,))],
    )(*results)
    return attended, query_grad, resp_grad[:, None], prompt_grad


def solution(mesh):
    return jax.shard_map(
        local,
        mesh=mesh,
        in_specs=(
            P("dp", "tensor"),
            P("dp", "tensor", None),
            P(("dp", "tensor"), None, None),
            P("dp", None),
            P("dp", None),
            P("dp", "tensor"),
        ),
        out_specs=(
            P("dp", "tensor"),
            P("dp", "tensor"),
            P("dp", "tensor", None),
            P(("dp", "tensor"), None, None),
        ),
        check_vma=False,
    )
```

time: 90.7 us -> 59.8 us (0.66)
  Pallas kernels: 83.8 us -> 58.9 us
  local copies, waits for them, and re-layouts: 5.06 us -> 0 us
  other arithmetic: 0.92 us -> 0 us
    pallas_call x1 -> x2, Pallas kernels: 83.8 us -> 58.9 us  [the longest x1 57 us: local(): pl.pallas_call(kernel, out_shape=shapes, in_specs=[anywhere] * 5 + [pl.Bl...]
    unnamed x11 -> x0, local copies, waits for them, and re-layouts: 5.06 us -> none
    convert_element_type x1 -> x0, other arithmetic: 0.92 us -> none  [local(): prompt_grad.transpose(1, 0, 2).astype(F32)]
where the time goes in v2:
time: 59.8 us; the launch traced here: 59.7 us
  Pallas kernels  58.9 us (98%)
  between operations  0.8 us (1%)
    pallas_call x1, Pallas kernels, local(): pl.pallas_call(kernel, out_shape=shapes, in_specs=[anywhere] * 5 + [pl.Bl...  57 us
    pallas_call x1, Pallas kernels, local(): pl.pallas_call(hand_on, out_shape=shapes, in_specs=[anywhere] * 4, out_sp...  1.92 us

profile of v2, /device:TPU:2, one launch (start us, length us, event | category | flops | bytes accessed | tf_op | source)
XLA Modules:
  0.0 59.7 jit_solution(7864525725494863381)
XLA Ops:
  0.6 57.0 %shard_map.93 = (bf16[128,1024]{1,0:T(8,128)(2,1)}, bf16[128,1024]{1,0:T(8,128)(2,1)}, bf16[128,256]{1,0:T(8,128)(2,1)}, f32[32,8,256]{2,1,0:T(8,128)}) custom-call(bf16[128,1024]{1,0:T(8,128)(2,1)} %q.1, bf16[128,1024]{1,0:T(8,128)(2,1)} %g.1, bf16[128,256]{1,0:T(8,128)(2,1)} %bitcast.2, bf16[32,8,256]{2,1,0:T(8,128)(2,1)} %pkv.1, s32[1,128]{1,0:T(1,128)} %seg.1, ...), custom_call_target="tpu_custom_call" | custom-call | tf_op jit(solution)/shard_map/pallas_call | solution.py:747
  57.6 1.9 %shard_map.94 = (bf16[128,1024]{1,0:T(8,128)(2,1)}, bf16[128,1024]{1,0:T(8,128)(2,1)}, bf16[128,256]{1,0:T(8,128)(2,1)}, f32[32,8,256]{2,1,0:T(8,128)}) custom-call(bf16[128,1024]{1,0:T(8,128)(2,1)} %get-tuple-element.12.refs_0_, bf16[128,1024]{1,0:T(8,128)(2,1)} %get-tuple-element.13.refs_1_, bf16[128,256]{1,0:T(8,128)(2,1)} %get-tuple-element.14.refs_2_, ...), custom_call_target="tpu_custom_call" | custom-call | tf_op jit(solution)/shard_map/pallas_call | solution.py:757

commit v3 on v2

--- a/solution.py
+++ b/solution.py
@@ -21,7 +21,6 @@
 OFFS = (0, 1, 7, 2, 6, 3, 5, 4)
 GATHER_MERGED = (1, 2)
 GATHER_RELAYED = (0, 1, 2, 3)
-SCATTER_RELAYED = ()
 SCATTER_MERGED = (1,)
 SCALE = 1.0 / math.sqrt(HD)
 ALPHA = SCALE * math.log2(math.e)
@@ -234,12 +233,20 @@
 )
 
 
+class Batch:
+    def __init__(self, whole, sem):
+        self.whole = pltpu.make_async_copy(whole, whole, sem)
+
+    def wait_recv(self):
+        self.whole.wait()
+
+
 class Net:
     def __init__(self, send_sem, recv_sem):
         self.dp, self.t = lax.axis_index("dp"), lax.axis_index("tensor")
         self.x, self.y, self.c = self.dp // 8, (self.dp // 2) % 4, self.dp % 2
         self.send_sem, self.recv_sem = send_sem, recv_sem
-        self.count = 0
+        self.count = self.taken = 0
         self.sent = []
 
     def at(self, axis):
@@ -251,16 +258,26 @@
         c = 1 - self.c if other else self.c
         return (x * 8 + y * 2 + c, (self.t + up) % 8)
 
-    def copy(self, src, dst, device):
+    def batch(self, whole, copies):
+        shared = self.taken
+        self.taken += 1
+        for src, dst, device in copies:
+            self.copy(src, dst, device, shared)
+        return Batch(whole, self.recv_sem.at[shared])
+
+    def copy(self, src, dst, device, shared=None):
         index = self.count
         self.count += 1
+        if shared is None:
+            shared = self.taken
+            self.taken += 1
         if index >= SENDS:
             self.sent[index - SENDS].wait_send()
         made = pltpu.make_async_remote_copy(
             src_ref=src,
             dst_ref=dst,
             send_sem=self.send_sem.at[index % SENDS],
-            recv_sem=self.recv_sem.at[index],
+            recv_sem=self.recv_sem.at[shared],
             device_id=device,
             device_id_type=MESH,
         )
@@ -318,16 +335,20 @@
         net = self.net
         return self.buf.at[net.x, net.y, net.c, pl.ds(self.low, SLAB)]
 
+    def row(self, src, count, devices):
+        whole = self.buf.at[0, 0:count, self.net.c, pl.ds(self.low, SLAB)]
+        return self.net.batch(whole, [(src, self.mine(), device) for device in devices])
+
     def up(self, slabs):
         net, place, axis = self.net, self.place, first_axis(self.place)
         away = -OFFS[place] % 8
         slab = slabs.at[(net.t + away) % 8]
-        self.arrived, self.lined = None, []
+        self.arrived = None
         if place == 0:
             self.buf[net.x, net.y, net.c, 0:SLAB] = slab[...]
-            self.lined = [net.copy(slab, self.mine(), net.device(axis, step)) for step in (1, 2, 3)]
+            self.lined = self.row(slab, 3, [net.device(axis, step) for step in (1, 2, 3)])
         elif place in GATHER_MERGED:
-            self.lined = [net.copy(slab, self.mine(), net.device(axis, step, away)) for step in (1, 2, 3, 0)]
+            self.lined = self.row(slab, 4, [net.device(axis, step, away) for step in (1, 2, 3, 0)])
         else:
             self.arrived = net.copy(slab, self.mine(), net.device(None, 0, away))
 
@@ -335,15 +356,17 @@
         if self.arrived is not None:
             net, axis = self.net, first_axis(self.place)
             self.arrived.wait_recv()
-            self.lined = [net.copy(self.mine(), self.mine(), net.device(axis, step)) for step in (1, 2, 3)]
+            self.lined = self.row(self.mine(), 3, [net.device(axis, step) for step in (1, 2, 3)])
 
     def second(self):
         net, axis = self.net, second_axis(self.place)
-        for made in self.lined:
-            made.wait_recv()
-        whole = self.line(axis, net.at(axis))
-        steps = (1, 3) if self.place in GATHER_RELAYED else (1, 2, 3)
-        self.lines = [net.copy(whole, whole, net.device(axis, step)) for step in steps]
+        self.lined.wait_recv()
+        line = self.line(axis, net.at(axis))
+        if self.place in GATHER_RELAYED:
+            self.lines = [net.copy(line, line, net.device(axis, step)) for step in (1, 3)]
+        else:
+            whole = self.buf.at[0:3, :, net.c, pl.ds(self.low, SLAB)]
+            self.lines = [net.batch(whole, [(line, line, net.device(axis, step)) for step in (1, 2, 3)])]
 
     def relay(self):
         if self.place in GATHER_RELAYED:
@@ -369,7 +392,6 @@
 class Scatter:
     def __init__(self, net, work, kind, j, refs, final, heads):
         self.net, self.work, self.kind, self.j, self.final, self.heads = net, work, kind, j, final, heads
-        self.relayed = f"{kind}{j}" in SCATTER_RELAYED
         self.__dict__.update(refs)
 
     def start(self):
@@ -384,8 +406,8 @@
         lax.fori_loop(0, 8, body, 0, unroll=4)
         self.sibling = net.copy(self.give, self.take, net.device(other=True))
 
-    def line(self, half, axis, at, low=0, size=SLAB):
-        rows = pl.ds(half * SLAB + low, size)
+    def line(self, half, axis, at):
+        rows = pl.ds(half * SLAB, SLAB)
         return self.held.at[at, :, rows] if axis == "x" else self.held.at[:, at, rows]
 
     def own(self):
@@ -403,44 +425,15 @@
         self.lined = []
         for half in (0, 1):
             axis = second_axis(half)
-            if self.relayed:
-                copies = []
-                for way, step in enumerate((1, 3)):
-                    part = pl.ds(way * (SLAB // 2), SLAB // 2)
-                    src = self.line(half, axis, (net.at(axis) + 2) % 4, way * (SLAB // 2), SLAB // 2)
-                    copies.append(net.copy(src, self.came.at[half, 2, :, part], net.device(axis, step)))
-                self.lined.append(copies)
-                continue
-            self.lined.append(
-                [
-                    net.copy(
-                        self.line(half, axis, (net.at(axis) + step) % 4),
-                        self.came.at[half, step - 1],
-                        net.device(axis, step),
-                    )
-                    for step in (1, 2, 3)
-                ]
-            )
-
-    def near(self):
-        if self.relayed:
-            net = self.net
-            far, self.lined = self.lined, []
-            for half in (0, 1):
-                axis = second_axis(half)
-                copies = []
-                for way, step in enumerate((1, 3)):
-                    far[half][way].wait_recv()
-                    mine = self.line(half, axis, (net.at(axis) + step) % 4)[...]
-                    part = slice(way * (SLAB // 2), (way + 1) * (SLAB // 2))
-                    rest = slice((1 - way) * (SLAB // 2), (2 - way) * (SLAB // 2))
-                    added = mine[:, part].astype(F32) + self.came[half, 2, :, part].astype(F32)
-                    self.handed[half, way, :, part] = added.astype(BF)
-                    self.handed[half, way, :, rest] = mine[:, rest]
-                    copies.append(
-                        net.copy(self.handed.at[half, way], self.came.at[half, way], net.device(axis, step))
-                    )
-                self.lined.append(copies)
+            copies = [
+                (
+                    self.line(half, axis, (net.at(axis) + step) % 4),
+                    self.came.at[half, step - 1],
+                    net.device(axis, step),
+                )
+                for step in (1, 2, 3)
+            ]
+            self.lined.append(net.batch(self.came.at[half], copies))
 
     def turn(self):
         net = self.net
@@ -448,8 +441,8 @@
         for half in (0, 1):
             axis = second_axis(half)
             total = self.line(half, axis, net.at(axis))[...].astype(F32)
-            for index, made in enumerate(self.lined[half]):
-                made.wait_recv()
+            self.lined[half].wait_recv()
+            for index in range(3):
                 total = total + self.came[half, index].astype(F32)
             self.rest[half] = total.astype(BF)
             place, axis = 2 * self.j + half, first_axis(half)
@@ -460,12 +453,12 @@
                 if away == 0 and step == 0:
                     self.final[place, 0] = src[...]
                 else:
-                    copies.append(net.copy(src, dst, net.device(axis, step, away)))
-            self.homeward.append(copies)
+                    copies.append((src, dst, net.device(axis, step, away)))
+            whole = self.final.at[place, 4 - len(copies) : 4]
+            self.homeward.append(net.batch(whole, copies))
 
     def summed(self, place, half):
-        for made in self.homeward[half]:
-            made.wait_recv()
+        self.homeward[half].wait_recv()
         total = self.final[place, 0].astype(F32)
         for step in (1, 2, 3):
             total = total + self.final[place, step].astype(F32)
@@ -500,15 +493,14 @@
     take=pltpu.VMEM((4, 4, BLK, HD), BF),
     held=pltpu.VMEM((4, 4, BLK, HD), BF),
     came=pltpu.VMEM((2, 3, 4, SLAB, HD), BF),
-    handed=pltpu.VMEM((2, 2, 4, SLAB, HD), BF),
     rest=pltpu.VMEM((2, 4, SLAB, HD), BF),
     ready=pltpu.VMEM((2, SLAB, HD), BF),
     came_up=pltpu.VMEM((2, SLAB, HD), BF),
 )
-COPIES = 252
+RECEIVES = 134
 SENDS = 64
 SCRATCH = (
-    [("send_sem", pltpu.SemaphoreType.DMA((SENDS,))), ("recv_sem", pltpu.SemaphoreType.DMA((COPIES,)))]
+    [("send_sem", pltpu.SemaphoreType.DMA((SENDS,))), ("recv_sem", pltpu.SemaphoreType.DMA((RECEIVES,)))]
     + [("kb", pltpu.VMEM((4, 4, 2, BLK, HD), BF)), ("vb", pltpu.VMEM((4, 4, 2, BLK, HD), BF))] * NCH
     + [("dk", pltpu.VMEM((RESP, 4, BLK, HD), BF)), ("dv", pltpu.VMEM((RESP, 4, BLK, HD), BF))] * NCH
     + [

time: 59.8 us -> 58.7 us (0.982)
  Pallas kernels: 58.9 us -> 57.8 us
    pallas_call x1, Pallas kernels: 57 us -> 55.9 us  [local(): pl.pallas_call(kernel, out_shape=shapes, in_specs=[anywhere] * 5 + [pl.Bl...]
where the time goes in v3:
time: 58.7 us; the launch traced here: 58.6 us
  Pallas kernels  57.8 us (98%)
  between operations  0.8 us (1%)
    pallas_call x1, Pallas kernels, local(): pl.pallas_call(kernel, out_shape=shapes, in_specs=[anywhere] * 5 + [pl.Bl...  55.9 us
    pallas_call x1, Pallas kernels, local(): pl.pallas_call(hand_on, out_shape=shapes, in_specs=[anywhere] * 4, out_sp...  1.92 us

profile of v3, /device:TPU:2, one launch (start us, length us, event | category | flops | bytes accessed | tf_op | source)
XLA Modules:
  0.0 58.6 jit_solution(9229460955407184102)
XLA Ops:
  0.6 55.9 %shard_map.93 = (bf16[128,1024]{1,0:T(8,128)(2,1)}, bf16[128,1024]{1,0:T(8,128)(2,1)}, bf16[128,256]{1,0:T(8,128)(2,1)}, f32[32,8,256]{2,1,0:T(8,128)}) custom-call(bf16[128,1024]{1,0:T(8,128)(2,1)} %q.1, bf16[128,1024]{1,0:T(8,128)(2,1)} %g.1, bf16[128,256]{1,0:T(8,128)(2,1)} %bitcast.2, bf16[32,8,256]{2,1,0:T(8,128)(2,1)} %pkv.1, s32[1,128]{1,0:T(1,128)} %seg.1, ...), custom_call_target="tpu_custom_call" | custom-call | tf_op jit(solution)/shard_map/pallas_call | solution.py:739
  56.5 1.9 %shard_map.94 = (bf16[128,1024]{1,0:T(8,128)(2,1)}, bf16[128,1024]{1,0:T(8,128)(2,1)}, bf16[128,256]{1,0:T(8,128)(2,1)}, f32[32,8,256]{2,1,0:T(8,128)}) custom-call(bf16[128,1024]{1,0:T(8,128)(2,1)} %get-tuple-element.12.refs_0_, bf16[128,1024]{1,0:T(8,128)(2,1)} %get-tuple-element.13.refs_1_, bf16[128,256]{1,0:T(8,128)(2,1)} %get-tuple-element.14.refs_2_, ...), custom_call_target="tpu_custom_call" | custom-call | tf_op jit(solution)/shard_map/pallas_call | solution.py:749

commit v4 on v3

--- a/solution.py
+++ b/solution.py
@@ -498,7 +498,7 @@
     came_up=pltpu.VMEM((2, SLAB, HD), BF),
 )
 RECEIVES = 134
-SENDS = 64
+SENDS = 32
 SCRATCH = (
     [("send_sem", pltpu.SemaphoreType.DMA((SENDS,))), ("recv_sem", pltpu.SemaphoreType.DMA((RECEIVES,)))]
     + [("kb", pltpu.VMEM((4, 4, 2, BLK, HD), BF)), ("vb", pltpu.VMEM((4, 4, 2, BLK, HD), BF))] * NCH

time: 58.7 us -> 58.5 us (level)
  no operation moved by 1% of the time
where the time goes in v4:
time: 58.5 us; the launch traced here: 58.3 us
  Pallas kernels  57.5 us (98%)
  between operations  0.8 us (1%)
    pallas_call x1, Pallas kernels, local(): pl.pallas_call(kernel, out_shape=shapes, in_specs=[anywhere] * 5 + [pl.Bl...  55.6 us
    pallas_call x1, Pallas kernels, local(): pl.pallas_call(hand_on, out_shape=shapes, in_specs=[anywhere] * 4, out_sp...  1.92 us

profile of v4, /device:TPU:2, one launch (start us, length us, event | category | flops | bytes accessed | tf_op | source)
XLA Modules:
  0.0 58.3 jit_solution(15937892223890284380)
XLA Ops:
  0.6 55.6 %shard_map.93 = (bf16[128,1024]{1,0:T(8,128)(2,1)}, bf16[128,1024]{1,0:T(8,128)(2,1)}, bf16[128,256]{1,0:T(8,128)(2,1)}, f32[32,8,256]{2,1,0:T(8,128)}) custom-call(bf16[128,1024]{1,0:T(8,128)(2,1)} %q.1, bf16[128,1024]{1,0:T(8,128)(2,1)} %g.1, bf16[128,256]{1,0:T(8,128)(2,1)} %bitcast.2, bf16[32,8,256]{2,1,0:T(8,128)(2,1)} %pkv.1, s32[1,128]{1,0:T(1,128)} %seg.1, ...), custom_call_target="tpu_custom_call" | custom-call | tf_op jit(solution)/shard_map/pallas_call | solution.py:739
  56.3 1.9 %shard_map.94 = (bf16[128,1024]{1,0:T(8,128)(2,1)}, bf16[128,1024]{1,0:T(8,128)(2,1)}, bf16[128,256]{1,0:T(8,128)(2,1)}, f32[32,8,256]{2,1,0:T(8,128)}) custom-call(bf16[128,1024]{1,0:T(8,128)(2,1)} %get-tuple-element.12.refs_0_, bf16[128,1024]{1,0:T(8,128)(2,1)} %get-tuple-element.13.refs_1_, bf16[128,256]{1,0:T(8,128)(2,1)} %get-tuple-element.14.refs_2_, ...), custom_call_target="tpu_custom_call" | custom-call | tf_op jit(solution)/shard_map/pallas_call | solution.py:749
